TPU v7x, 256 devices: a whole 4x4x8 slice. The times are simulated.
256 devices in a mesh: rows: 64 (over z, y, core), batch: 4 (over x).
Axes of the slice: x: 4, y: 4, z: 8, core: 2. Of those that a mesh axis runs over, the one named last changes fastest.
Arguments:
- velocity: bfloat16 [8, 131072, 512], P(None, 'rows', 'batch'), may hold values from -48 to 48, as said below
Outputs:
- factor: float32 [8, 128, 128], replicated
- modes: float32 [8, 131072, 512], P(None, 'rows', 'batch')
Inputs may be any that keep to these rules, and one draw needn't show every extreme that they name: velocity values of every plane, with nonzero spread in every window.
All inputs are finite; a program needn't handle non-finite values.
Results may differ from a plain program's by a relative error of at most 0.0003.
Values sent between devices are 32-bit elements; how exact they have to be, the bound alone decides.
No kernel may reach another device: no remote copies, remote signals or barrier semaphores. Data moves between devices by JAX's collectives and lax.ppermute only.
A program may use at most 128 MiB of HBM per device.

v0:
```python
import jax
import jax.numpy as jnp
from jax import lax
from jax.sharding import PartitionSpec as P


def upper_factor(gram):
    planes, width, _ = gram.shape
    places = jnp.arange(width, dtype=jnp.int32)

    def column_step(column, lower):
        row_part = lax.dynamic_slice_in_dim(lower, column, 1, 1)[:, 0, :]
        gram_col = lax.dynamic_slice_in_dim(gram, column, 1, 2)[:, :, 0]
        current = gram_col - jnp.einsum(
            "pik,pk->pi", lower, row_part, precision=lax.Precision.HIGHEST
        )
        pivot = lax.dynamic_slice_in_dim(current, column, 1, 1)
        root = jnp.sqrt(pivot)
        below = (places > column)[None, :]
        at_pivot = (places == column)[None, :]
        new_col = jnp.where(below, current / root, jnp.where(at_pivot, root, 0.0))
        return lax.dynamic_update_slice_in_dim(lower, new_col[:, :, None], column, 2)

    lower = lax.fori_loop(0, width, column_step, jnp.zeros((planes, width, width), jnp.float32))
    return jnp.swapaxes(lower, 1, 2)


def upper_inverse(factor):
    planes, width, _ = factor.shape
    places = jnp.arange(width, dtype=jnp.int32)

    def row_step(turn, result):
        index = width - 1 - turn
        factor_row = lax.dynamic_slice_in_dim(factor, index, 1, 1)[:, 0, :]
        pivot = lax.dynamic_slice_in_dim(factor_row, index, 1, 1)
        unit = (places == index).astype(jnp.float32)[None, :]
        solved = (
            unit - jnp.einsum("pk,pkj->pj", factor_row, result, precision=lax.Precision.HIGHEST)
        ) / pivot
        return lax.dynamic_update_slice_in_dim(result, solved[:, None, :], index, 1)

    return lax.fori_loop(0, width, row_step, jnp.zeros((planes, width, width), jnp.float32))


def shards(velocity):
    planes, rows_dev, width = velocity.shape
    stack = rows_dev * lax.axis_size("rows") * lax.axis_size("batch")
    local_gram = jnp.einsum("prk,prj->pkj", velocity, velocity, preferred_element_type=jnp.float32)
    total_gram = lax.psum(local_gram, ("rows", "batch"))
    raw_factor = upper_factor(total_gram)
    factor = raw_factor / jnp.sqrt(jnp.float32(stack))
    inverse = upper_inverse(factor)
    modes = jnp.einsum(
        "prk,pkj->prj",
        velocity,
        inverse,
        precision=lax.Precision.HIGHEST,
        preferred_element_type=jnp.float32,
    )
    return (factor, modes)


def solution(mesh):
    placed = (P(None, "rows", "batch"),)
    return jax.shard_map(
        shards,
        mesh=mesh,
        in_specs=placed,
        out_specs=(P(), P(None, "rows", "batch")),
        check_vma=False,
    )
```

profile of v0, /device:TPU:1, one launch (start us, length us, event | category | flops | bytes accessed | tf_op | source)
XLA Modules:
  0.0 1531.1 jit_solution(10900084931543123307)
XLA Ops:
  7.2 5.6 fusion.7
  12.8 255.7 %all-reduce.2.cloned.1.call-done = f32[8,128,128]{2,1,0:T(8,128)} async-done(((f32[8,128,128]{2,1,0:T(8,128)}), f32[8,128,128]{2,1,0:T(8,128)}) %all-reduce.2.cloned.1.call-update) | async-done | bytes 524304 | tf_op jit(solution)/shard_map/psum | solution.py:49
  268.5 8.3 copy.4
  281.3 923.7 %while.33 = (s32[]{:T(128)}, f32[8,128,128]{0,1,2:T(8,128)}, f32[8,128,128]{0,1,2:T(8,128)}, s32[]{:T(128)}) while((s32[]{:T(128)}, f32[8,128,128]{0,1,2:T(8,128)}, f32[8,128,128]{0,1,2:T(8,128)}, s32[]{:T(128)}) %tuple.81), condition=%wide.region_2.3_spmd.clone.clone, body=%wide.region_1.2_spmd.clone.clone.sunk | while | flops 265474 | bytes 623781 | solution.py:24
  296.8 4.5 multiply_reduce_fusion.2
  304.0 4.5 multiply_reduce_fusion.2
  332.9 4.5 multiply_reduce_fusion.2
  340.1 4.5 multiply_reduce_fusion.2
  361.7 4.5 multiply_reduce_fusion.2
  369.0 4.5 multiply_reduce_fusion.2
  376.2 4.5 multiply_reduce_fusion.2
  397.8 4.5 multiply_reduce_fusion.2
  405.0 4.5 multiply_reduce_fusion.2
  433.9 4.5 multiply_reduce_fusion.2
  441.1 4.5 multiply_reduce_fusion.2
  470.0 4.5 multiply_reduce_fusion.2
  477.2 4.5 multiply_reduce_fusion.2
  498.9 4.5 multiply_reduce_fusion.2
  506.1 4.5 multiply_reduce_fusion.2
  513.3 4.5 multiply_reduce_fusion.2
  534.9 4.5 multiply_reduce_fusion.2
  542.2 4.5 multiply_reduce_fusion.2
  571.0 4.5 multiply_reduce_fusion.2
  578.2 4.5 multiply_reduce_fusion.2
  607.1 4.5 multiply_reduce_fusion.2
  614.3 4.5 multiply_reduce_fusion.2
  636.0 4.5 multiply_reduce_fusion.2
  1205.0 5.1 copy.5
  1210.2 4.6 copy.7
  1214.8 291.5 %while.32 = (s32[]{:T(128)}, f32[8,128,128]{2,1,0:T(8,128)S(1)}, f32[8,128,128]{0,2,1:T(8,128)}, s32[]{:T(128)}, s32[]{:T(128)}, /*index=5*/s32[]{:T(128)}, s32[]{:T(128)}) while((s32[]{:T(128)}, f32[8,128,128]{2,1,0:T(8,128)S(1)}, f32[8,128,128]{0,2,1:T(8,128)}, s32[]{:T(128)}, s32[]{:T(128)}, /*index=5*/s32[]{:T(128)}, ...), condition=%wide.region_4.5_spmd.clone, body=%wide.region_3.4_spmd.clone.sunk | while | flops 1575175 | bytes 566523 | solution.py:42
  1506.3 8.9 convolution_bitcast_fusion
  1515.2 9.1 copy.9
  (1648 shorter events, 1110.2 us)
Async XLA Ops:
  7.2 261.3 %all-reduce.2.cloned.1.call-start = ((), (), s32[]{:S(2)}) async-start(), calls=%async_computation | async-start | bytes 1048576 | tf_op jit(solution)/shard_map/psum | solution.py:49
  1210.2 305.0 %copy-start = (f32[8,128,128]{2,1,0:T(8,128)}, f32[8,128,128]{2,1,0:T(8,128)S(1)}, u32[]{:S(2)}) copy-start(f32[8,128,128]{2,1,0:T(8,128)S(1)} %multiply_bitcast_fusion) | copy-start | bytes 1572868
Sparse Core Ops, SparseCore 0:
  14.0 254.4 all-reduce.1
where the time goes:
time: 1560 us; the launch traced here: 1530 us
  other arithmetic  791 us (51%)
  local copies, waits for them, and re-layouts  380 us (24%)
  waiting for transfers between devices  256 us (16%)
  matrix products  84.2 us (5%)
    dot_general x128, other arithmetic, column_step(): jnp.einsum('pik,pk->pi', lower, row_part, precision=lax.Precision.HIGHEST)  577 us
    psum x1, waiting for transfers between devices, shards(): total_gram = lax.psum(local_gram, ('rows', 'batch'))  256 us
    dynamic_slice x128, local copies, waits for them, and re-layouts, column_step(): row_part = lax.dynamic_slice_in_dim(lower, column, 1, 1)[:, 0, :]  139 us
    squeeze x256, local copies, waits for them, and re-layouts, row_step(): factor_row = lax.dynamic_slice_in_dim(factor, index, 1, 1)[:, 0, :]  115 us
    sub x128, other arithmetic, column_step(): gram_col - jnp.einsum('pik,pk->pi', lower, row_part, precision=lax.Precis...  109 us
    dynamic_update_slice x128, other arithmetic, column_step(): lax.dynamic_update_slice_in_dim(lower, new_col[:, :, None], column, 2)  94.5 us
    div x128, local copies, waits for them, and re-layouts, row_step(): (unit - jnp.einsum('pk,pkj->pj', factor_row, result, precision=lax.Precis...  89.5 us
    dot_general x128, matrix products, row_step(): jnp.einsum('pk,pkj->pj', factor_row, result, precision=lax.Precision.HIGH...  69.7 us
  transfers between devices with their start and end apart: 1, of which 1 were waited for; matrix products, arithmetic and copies ran while one was open for 0% of the time, Pallas kernels for 0%

commit v1 on v0

v1 whole, which is shorter than its diff:
```python
import jax
import jax.numpy as jnp
from jax import lax
from jax.experimental import pallas as pl
from jax.experimental.pallas import tpu as pltpu
from jax.sharding import PartitionSpec as P

BLOCK = 8
GROUP = 16
TILE = 512
LIMIT = 40 * 1024 * 1024


def packing(width):
    groups = width // GROUP
    half = groups // 2
    place = {}
    for a in range(half):
        for r in range(GROUP):
            place[a * GROUP + r] = (a * GROUP + r, 0)
            if a:
                place[(groups - a) * GROUP + r] = (a * GROUP + r, a * GROUP)
    for r in range(GROUP // 2):
        at = half * GROUP + r
        place[at] = (at, 0)
        place[at + GROUP // 2] = (at, width // 2)
    return place, half * GROUP + GROUP // 2


def gram_kernel(planes, width, v_ref, packed_ref, gram_ref):
    p = pl.program_id(0)
    v = v_ref[0]
    gram_ref[pl.ds(p, width, stride=planes), :] = lax.dot_general(
        v, v, (((0,), (0,)), ((), ())), preferred_element_type=jnp.float32
    )

    @pl.when(p == planes - 1)
    def _():
        place, _ = packing(width)
        lanes = lax.broadcasted_iota(jnp.int32, (planes, width), 1)
        for row, (at, roll) in place.items():
            if roll:
                continue
            value = gram_ref[row * planes : (row + 1) * planes, :]
            for other, (other_at, other_roll) in place.items():
                if other_at == at and other_roll:
                    moved = pltpu.roll(gram_ref[other * planes : (other + 1) * planes, :], other_roll, 1)
                    value = jnp.where(lanes < other_roll, moved, value)
            packed_ref[at * planes : (at + 1) * planes, :] = value


def lane(value, j):
    return jnp.broadcast_to(value[:, j : j + 1], value.shape)


def factor_rows(scale, packed_ref, u_ref, p_ref, width, planes):
    place, _ = packing(width)
    lanes = lax.broadcasted_iota(jnp.int32, (planes, width), 1)

    def given(i):
        at, roll = place[i]
        row = packed_ref[at * planes : (at + 1) * planes, :]
        return (pltpu.roll(row, width - roll, 1) if roll else row) * scale

    for start in range(0, width, BLOCK):
        inside = (lanes >= start) & (lanes < start + BLOCK)
        rows = [jnp.where(lanes >= start, given(start + i), 0.0) for i in range(BLOCK)]

        def older(k, rows):
            rows = list(rows)
            at = pl.ds(pl.multiple_of(k * planes, planes), planes)
            source = p_ref[at, :]
            for i in range(BLOCK):
                rows[i] = rows[i] - lane(source, start + i) * source
            p_ref[at, :] = jnp.where(inside, 0.0, source)
            return tuple(rows)

        if start:
            rows = list(lax.fori_loop(0, start, older, tuple(rows), unroll=8))
        cell = {(i, j): lane(rows[i], start + j) for i in range(BLOCK) for j in range(i, BLOCK)}
        for k in range(BLOCK):
            pivot = cell[k, k]
            root = lax.rsqrt(pivot)
            root = root * (1.5 - 0.5 * pivot * root * root)
            for j in range(k + 1, BLOCK):
                cell[k, j] = cell[k, j] * root
            for i in range(k + 1, BLOCK):
                for j in range(i, BLOCK):
                    cell[i, j] = cell[i, j] - cell[k, i] * cell[k, j]
            here = lanes == start + k
            whole = rows[k] * root
            u_ref[pl.ds(start + k, planes, stride=width), :] = jnp.where(lanes >= start + k, whole, 0.0)
            whole = jnp.where(here, root, whole)
            p_ref[(start + k) * planes : (start + k + 1) * planes, :] = jnp.where(
                (lanes <= start + k) | (lanes >= start + BLOCK), whole, 0.0
            )
            for i in range(k + 1, BLOCK):
                rows[i] = jnp.where(here, 0.0, rows[i]) - cell[k, i] * whole


def modes_kernel(scale, planes, width, packed_ref, v_hbm, u_ref, m_hbm, p_ref, v_ref, m_ref, in_sem, out_sem):
    def fetch(p):
        return pltpu.make_async_copy(v_hbm.at[p], v_ref.at[p], in_sem.at[p])

    def put(p):
        return pltpu.make_async_copy(m_ref.at[p], m_hbm.at[p], out_sem.at[p])

    for p in range(planes):
        fetch(p).start()
    factor_rows(scale, packed_ref, u_ref, p_ref, width, planes)
    rows_dev = v_ref.shape[1]
    for p in range(planes):
        rest = p_ref[pl.ds(p, width, stride=planes), :]
        high = rest.astype(jnp.bfloat16)
        rest = rest - high.astype(jnp.float32)
        middle = rest.astype(jnp.bfloat16)
        low = (rest - middle.astype(jnp.float32)).astype(jnp.bfloat16)
        weights = jnp.concatenate(
            [
                jnp.concatenate([high, middle], axis=1),
                jnp.concatenate([low, jnp.zeros_like(low)], axis=1),
            ],
            axis=0,
        )
        fetch(p).wait()

        def tile(t, _):
            at = pl.ds(pl.multiple_of(t * TILE, TILE), TILE)
            v = v_ref[p, at, :]
            both = lax.dot_general(
                jnp.concatenate([v, v], axis=1),
                weights,
                (((1,), (1,)), ((), ())),
                preferred_element_type=jnp.float32,
            )
            m_ref[p, at, :] = both[:, :width] + both[:, width:]
            return 0

        lax.fori_loop(0, rows_dev // TILE, tile, 0)
        put(p).start()
    for p in range(planes):
        put(p).wait()


def index(z, y, core):
    return (z * 4 + y) * 2 + core


def rows_perm(move):
    return [(index(z, y, c), index(*move(z, y, c))) for z in range(8) for y in range(4) for c in range(2)]


def total(x):
    core = lax.axis_index("rows") % 2
    here = lax.axis_index("batch")
    other_core = rows_perm(lambda z, y, c: (z, y, 1 - c))
    n = x.shape[0] // 2
    x = lax.dynamic_slice_in_dim(x, core * n, n, 0) + lax.ppermute(
        lax.dynamic_slice_in_dim(x, (1 - core) * n, n, 0), "rows", other_core
    )
    m = n // 4
    shift = {d: [(i, (i + d) % 4) for i in range(4)] for d in (1, 2, 3)}
    got = [
        lax.ppermute(lax.dynamic_slice_in_dim(x, ((here + d) % 4) * m, m, 0), "batch", shift[d]) for d in (1, 2, 3)
    ]
    x = lax.dynamic_slice_in_dim(x, here * m, m, 0) + got[0] + got[1] + got[2]
    got = [lax.ppermute(x, "rows", rows_perm(lambda z, y, c: (z, (y + d) % 4, c))) for d in (1, 2, 3)]
    x = (x + got[1]) + (got[0] + got[2])
    for bit in (1, 2, 4):
        x = x + lax.ppermute(x, "rows", rows_perm(lambda z, y, c: (z ^ bit, y, c)))
    got = [x] + [lax.ppermute(x, "batch", shift[d]) for d in (1, 2, 3)]
    x = jnp.concatenate(
        [
            jnp.where(
                here == j,
                got[0],
                jnp.where(here == (j + 1) % 4, got[1], jnp.where(here == (j + 2) % 4, got[2], got[3])),
            )
            for j in range(4)
        ],
        axis=0,
    )
    y = lax.ppermute(x, "rows", other_core)
    return jnp.concatenate([jnp.where(core == 0, x, y), jnp.where(core == 0, y, x)], axis=0)


def shards(velocity):
    planes, rows_dev, width = velocity.shape
    stack = rows_dev * lax.axis_size("rows") * lax.axis_size("batch")
    _, packed_rows = packing(width)
    packed = pl.pallas_call(
        lambda *refs: gram_kernel(planes, width, *refs),
        grid=(planes,),
        in_specs=[pl.BlockSpec((1, rows_dev, width), lambda p: (p, 0, 0))],
        out_specs=pl.BlockSpec((packed_rows * planes, width), lambda p: (0, 0)),
        out_shape=jax.ShapeDtypeStruct((packed_rows * planes, width), jnp.float32),
        scratch_shapes=[pltpu.VMEM((width * planes, width), jnp.float32)],
        compiler_params=pltpu.CompilerParams(vmem_limit_bytes=LIMIT),
        name="gram",
    )(velocity)
    packed = total(packed)
    factor, modes = pl.pallas_call(
        lambda *refs: modes_kernel(1.0 / stack, planes, width, *refs),
        in_specs=[pl.BlockSpec(memory_space=pltpu.VMEM), pl.BlockSpec(memory_space=pl.ANY)],
        out_specs=[pl.BlockSpec(memory_space=pltpu.VMEM), pl.BlockSpec(memory_space=pl.ANY)],
        out_shape=[
            jax.ShapeDtypeStruct((planes * width, width), jnp.float32),
            jax.ShapeDtypeStruct((planes, rows_dev, width), jnp.float32),
        ],
        scratch_shapes=[
            pltpu.VMEM((width * planes, width), jnp.float32),
            pltpu.VMEM((planes, rows_dev, width), jnp.bfloat16),
            pltpu.VMEM((planes, rows_dev, width), jnp.float32),
            pltpu.SemaphoreType.DMA((planes,)),
            pltpu.SemaphoreType.DMA((planes,)),
        ],
        compiler_params=pltpu.CompilerParams(vmem_limit_bytes=LIMIT),
        name="factor_modes",
    )(packed, velocity)
    return (factor.reshape(planes, width, width), modes)


def solution(mesh):
    placed = (P(None, "rows", "batch"),)
    return jax.shard_map(
        shards,
        mesh=mesh,
        in_specs=placed,
        out_specs=(P(), P(None, "rows", "batch")),
        check_vma=False,
    )
```

time: 1560 us -> 91.4 us (0.06); the launches traced: 1530 us -> 91.3 us
  other arithmetic: 791 us -> 0.14 us
  local copies, waits for them, and re-layouts: 380 us -> 4.4 us
  waiting for transfers between devices: 256 us -> 18.1 us
  matrix products: 84.2 us -> 0 us
  Pallas kernels: 0 us -> 37.8 us
  starting transfers between devices: 0.04 us -> 29.9 us
    dot_general x128 -> x0, other arithmetic: 577 us -> none  [column_step(): jnp.einsum('pik,pk->pi', lower, row_part, precision=lax.Precision.HIGHEST)]
    psum x1 -> x0, waiting for transfers between devices: 256 us -> none  [shards(): total_gram = lax.psum(local_gram, ('rows', 'batch'))]
    dynamic_slice x128 -> x2, local copies, waits for them, and re-layouts: 139 us -> 0.04 us  [the longest x1 0.02 us: total(): lax.dynamic_slice_in_dim(x, (here + d) % 4 * m, m, 0)]
    squeeze x256 -> x0, local copies, waits for them, and re-layouts: 115 us -> none  [row_step(): factor_row = lax.dynamic_slice_in_dim(factor, index, 1, 1)[:, 0, :]]
    sub x128 -> x0, other arithmetic: 109 us -> none  [column_step(): gram_col - jnp.einsum('pik,pk->pi', lower, row_part, precision=lax.Precis...]
    dynamic_update_slice x128 -> x0, other arithmetic: 94.5 us -> none  [column_step(): lax.dynamic_update_slice_in_dim(lower, new_col[:, :, None], column, 2)]
    div x256 -> x0, local copies, waits for them, and re-layouts: 90.6 us -> none  [the longest x128 89.5 us: row_step(): (unit - jnp.einsum('pk,pkj->pj', factor_row, result, precision=lax.Precis...]
    dot_general x130 -> x0, matrix products: 84.2 us -> none  [the longest x128 69.7 us: row_step(): jnp.einsum('pk,pkj->pj', factor_row, result, precision=lax.Precision.HIGH...]
  transfers between devices with their start and end apart: 1 -> 14, of which waited for: 1 -> 13; matrix products, arithmetic and copies ran while one was open for 0% -> 0% of each run, Pallas kernels for 0% -> 0%
where the time goes in v1:
time: 91.4 us; the launch traced here: 91.3 us
  Pallas kernels  37.8 us (41%)
  starting transfers between devices  29.9 us (33%)
  waiting for transfers between devices  18.1 us (20%)
  local copies, waits for them, and re-layouts  4.4 us (5%)
    pallas_call x1, Pallas kernels, shards(): pl.pallas_call(lambda *refs: modes_kernel(1.0 / stack, planes, width, *re...  34.9 us
    ppermute x3, starting transfers between devices, total(): x = x + lax.ppermute(x, 'rows', rows_perm(lambda z, y, c: (z ^ bit, y, c)))  10.1 us
    ppermute x1, starting transfers between devices, total(): y = lax.ppermute(x, 'rows', other_core)  8.66 us
    ppermute x3, waiting for transfers between devices, total(): x = x + lax.ppermute(x, 'rows', rows_perm(lambda z, y, c: (z ^ bit, y, c)))  4.55 us
    unnamed x4, local copies, waits for them, and re-layouts  4.37 us
    ppermute x3, waiting for transfers between devices, total(): lax.ppermute(lax.dynamic_slice_in_dim(x, (here + d) % 4 * m, m, 0), 'batc...  4.31 us
    ppermute x3, waiting for transfers between devices, total(): got = [x] + [lax.ppermute(x, 'batch', shift[d]) for d in (1, 2, 3)]  4.07 us
    ppermute x1, starting transfers between devices, total(): lax.ppermute(lax.dynamic_slice_in_dim(x, (1 - core) * n, n, 0), 'rows', o...  3.33 us
  transfers between devices with their start and end apart: 14, of which 13 were waited for; matrix products, arithmetic and copies ran while one was open for 0% of the time, Pallas kernels for 0%

profile of v1, /device:TPU:1, one launch (start us, length us, event | category | flops | bytes accessed | tf_op | source)
XLA Modules:
  0.0 91.3 jit_solution(5677529402300337220)
XLA Ops:
  0.6 0.0 copy-start
  0.7 2.2 %copy-done = bf16[8,2048,128]{2,1,0:T(8,128)(2,1)S(1)} copy-done((bf16[8,2048,128]{2,1,0:T(8,128)(2,1)S(1)}, bf16[8,2048,128]{2,1,0:T(8,128)(2,1)}, u32[]{:S(2)}) %copy-start) | copy-done | bytes 4194328
  2.8 2.9 %gram.1 = f32[576,128]{1,0:T(8,128)S(1)} custom-call(bf16[8,2048,128]{2,1,0:T(8,128)(2,1)S(1)} %copy-done), custom_call_target="tpu_custom_call" | custom-call | tf_op jit(solution)/shard_map/gram/pallas_call | solution.py:191
  5.8 3.3 %collective-permute-start = (f32[288,128]{1,0:T(8,128)S(1)}, f32[288,128]{1,0:T(8,128)S(1)}, u32[]{:S(2)}, u32[]{:S(2)}) collective-permute-start(f32[288,128]{1,0:T(8,128)S(1)} %constant_dynamic-slice_fusion.3), channel_id=1, source_target_pairs={{0,4},{4,0},{8,12},{12,8},{16,20},{20,16},{24,28},{28,24},{32,36},... | collective-permute-start | bytes 442376 | tf_op jit(solution)/shard_map/ppermute | solution.py:158
  9.1 1.0 %collective-permute-done = f32[288,128]{1,0:T(8,128)S(1)} collective-permute-done((f32[288,128]{1,0:T(8,128)S(1)}, f32[288,128]{1,0:T(8,128)S(1)}, u32[]{:S(2)}, u32[]{:S(2)}) %collective-permute-start) | collective-permute-done | bytes 147488 | tf_op jit(solution)/shard_map/ppermute | solution.py:158
  10.2 0.1 collective-permute-start.1
  10.3 2.7 %collective-permute-start.3 = (f32[72,128]{1,0:T(8,128)S(1)}, f32[72,128]{1,0:T(8,128)S(1)}, u32[]{:S(2)}, u32[]{:S(2)}) collective-permute-start(f32[72,128]{1,0:T(8,128)S(1)} %get-tuple-element.13), channel_id=1, source_target_pairs={{0,3},{1,0},{2,1},{3,2},{4,7},{5,4},{6,5},{7,6},{8,11},{9,8},{10,9... | collective-permute-start | bytes 110600 | tf_op jit(solution)/shard_map/ppermute | solution.py:164
  12.9 1.3 %collective-permute-done.1 = f32[72,128]{1,0:T(8,128)S(1)} collective-permute-done((f32[72,128]{1,0:T(8,128)S(1)}, f32[72,128]{1,0:T(8,128)S(1)}, u32[]{:S(2)}, u32[]{:S(2)}) %collective-permute-start.1) | collective-permute-done | bytes 36896 | tf_op jit(solution)/shard_map/ppermute | solution.py:164
  14.3 3.0 %collective-permute-done.2 = f32[72,128]{1,0:T(8,128)S(1)} collective-permute-done((f32[72,128]{1,0:T(8,128)S(1)}, f32[72,128]{1,0:T(8,128)S(1)}, u32[]{:S(2)}, u32[]{:S(2)}) %collective-permute-start.2) | collective-permute-done | bytes 36896 | tf_op jit(solution)/shard_map/ppermute | solution.py:164
  17.3 1.1 %collective-permute-start.6 = (f32[72,128]{1,0:T(8,128)S(1)}, f32[72,128]{1,0:T(8,128)S(1)}, u32[]{:S(2)}, u32[]{:S(2)}) collective-permute-start(f32[72,128]{1,0:T(8,128)S(1)} %add_add_fusion.1), channel_id=1, source_target_pairs={{0,24},{4,28},{8,0},{12,4},{16,8},{20,12},{24,16},{28,20},{32,56},... | collective-permute-start | bytes 110600 | tf_op jit(solution)/shard_map/ppermute | solution.py:167
  18.3 0.5 collective-permute-start.5
  18.8 1.2 %collective-permute-start.4 = (f32[72,128]{1,0:T(8,128)S(1)}, f32[72,128]{1,0:T(8,128)S(1)}, u32[]{:S(2)}, u32[]{:S(2)}) collective-permute-start(f32[72,128]{1,0:T(8,128)S(1)} %add_add_fusion.1), channel_id=1, source_target_pairs={{0,16},{4,20},{8,24},{12,28},{16,0},{20,4},{24,8},{28,12},{32,48},... | collective-permute-start | bytes 110600 | tf_op jit(solution)/shard_map/ppermute | solution.py:167
  20.0 0.2 collective-permute-done.6
  20.1 2.2 %collective-permute-done.5 = f32[72,128]{1,0:T(8,128)S(1)} collective-permute-done((f32[72,128]{1,0:T(8,128)S(1)}, f32[72,128]{1,0:T(8,128)S(1)}, u32[]{:S(2)}, u32[]{:S(2)}) %collective-permute-start.5) | collective-permute-done | bytes 36896 | tf_op jit(solution)/shard_map/ppermute | solution.py:167
  22.4 0.8 collective-permute-done.4
  23.1 1.4 %collective-permute-start.7 = (f32[72,128]{1,0:T(8,128)S(1)}, f32[72,128]{1,0:T(8,128)S(1)}, u32[]{:S(2)}, u32[]{:S(2)}) collective-permute-start(f32[72,128]{1,0:T(8,128)S(1)} %add_add_fusion), channel_id=1, source_target_pairs={{0,32},{4,36},{8,40},{12,44},{16,48},{20,52},{24,56},{28,60},{32,0... | collective-permute-start | bytes 110600 | tf_op jit(solution)/shard_map/ppermute | solution.py:170
  24.5 1.8 %collective-permute-done.7 = f32[72,128]{1,0:T(8,128)S(1)} collective-permute-done((f32[72,128]{1,0:T(8,128)S(1)}, f32[72,128]{1,0:T(8,128)S(1)}, u32[]{:S(2)}, u32[]{:S(2)}) %collective-permute-start.7) | collective-permute-done | bytes 36896 | tf_op jit(solution)/shard_map/ppermute | solution.py:170
  26.3 2.5 %collective-permute-start.8 = (f32[72,128]{1,0:T(8,128)S(1)}, f32[72,128]{1,0:T(8,128)S(1)}, u32[]{:S(2)}, u32[]{:S(2)}) collective-permute-start(f32[72,128]{1,0:T(8,128)S(1)} %add.90), channel_id=1, source_target_pairs={{0,64},{4,68},{8,72},{12,76},{16,80},{20,84},{24,88},{28,92},{32,9... | collective-permute-start | bytes 110600 | tf_op jit(solution)/shard_map/ppermute | solution.py:170
  28.8 1.4 %collective-permute-done.8 = f32[72,128]{1,0:T(8,128)S(1)} collective-permute-done((f32[72,128]{1,0:T(8,128)S(1)}, f32[72,128]{1,0:T(8,128)S(1)}, u32[]{:S(2)}, u32[]{:S(2)}) %collective-permute-start.8) | collective-permute-done | bytes 36896 | tf_op jit(solution)/shard_map/ppermute | solution.py:170
  30.2 6.2 %collective-permute-start.9 = (f32[72,128]{1,0:T(8,128)S(1)}, f32[72,128]{1,0:T(8,128)S(1)}, u32[]{:S(2)}, u32[]{:S(2)}) collective-permute-start(f32[72,128]{1,0:T(8,128)S(1)} %add.91), channel_id=1, source_target_pairs={{0,128},{4,132},{8,136},{12,140},{16,144},{20,148},{24,152},{28,15... | collective-permute-start | bytes 110600 | tf_op jit(solution)/shard_map/ppermute | solution.py:170
  36.4 1.3 %collective-permute-done.9 = f32[72,128]{1,0:T(8,128)S(1)} collective-permute-done((f32[72,128]{1,0:T(8,128)S(1)}, f32[72,128]{1,0:T(8,128)S(1)}, u32[]{:S(2)}, u32[]{:S(2)}) %collective-permute-start.9) | collective-permute-done | bytes 36896 | tf_op jit(solution)/shard_map/ppermute | solution.py:170
  37.8 1.3 %collective-permute-start.12 = (f32[72,128]{1,0:T(8,128)S(1)}, f32[72,128]{1,0:T(8,128)S(1)}, u32[]{:S(2)}, u32[]{:S(2)}) collective-permute-start(f32[72,128]{1,0:T(8,128)S(1)} %add.92), channel_id=1, source_target_pairs={{0,3},{1,0},{2,1},{3,2},{4,7},{5,4},{6,5},{7,6},{8,11},{9,8},{10,9... | collective-permute-start | bytes 110600 | tf_op jit(solution)/shard_map/ppermute | solution.py:171
  39.0 0.9 collective-permute-start.11
  39.9 0.2 collective-permute-start.10
  40.2 0.4 collective-permute-done.12
  40.6 2.8 %collective-permute-done.11 = f32[72,128]{1,0:T(8,128)S(1)} collective-permute-done((f32[72,128]{1,0:T(8,128)S(1)}, f32[72,128]{1,0:T(8,128)S(1)}, u32[]{:S(2)}, u32[]{:S(2)}) %collective-permute-start.11) | collective-permute-done | bytes 36896 | tf_op jit(solution)/shard_map/ppermute | solution.py:171
  43.3 0.9 collective-permute-done.10
  44.3 8.7 %collective-permute-start.13 = (f32[288,128]{1,0:T(8,128)S(1)}, f32[288,128]{1,0:T(8,128)S(1)}, u32[]{:S(2)}, u32[]{:S(2)}) collective-permute-start(f32[288,128]{1,0:T(8,128)S(1)} %pad_maximum_fusion.1), channel_id=1, source_target_pairs={{0,4},{4,0},{8,12},{12,8},{16,20},{20,16},{24,28},{28,24},{32,36},... | collective-permute-start | bytes 442376 | tf_op jit(solution)/shard_map/ppermute | solution.py:183
  52.9 1.0 %collective-permute-done.13 = f32[288,128]{1,0:T(8,128)S(1)} collective-permute-done((f32[288,128]{1,0:T(8,128)S(1)}, f32[288,128]{1,0:T(8,128)S(1)}, u32[]{:S(2)}, u32[]{:S(2)}) %collective-permute-start.13) | collective-permute-done | bytes 147488 | tf_op jit(solution)/shard_map/ppermute | solution.py:183
  54.0 0.0 copy-start.1
  54.0 2.2 %copy-done.1 = bf16[8,2048,128]{2,1,0:T(8,128)(2,1)S(1)} copy-done((bf16[8,2048,128]{2,1,0:T(8,128)(2,1)S(1)}, bf16[8,2048,128]{2,1,0:T(8,128)(2,1)}, u32[]{:S(2)}) %copy-start.1) | copy-done | bytes 4194328
  56.2 34.9 %factor_modes.1 = (f32[1024,128]{1,0:T(8,128)}, f32[8,2048,128]{2,1,0:T(8,128)}) custom-call(f32[576,128]{1,0:T(8,128)S(1)} %pad_maximum_fusion.refs_0_, bf16[8,2048,128]{2,1,0:T(8,128)(2,1)S(1)} %copy-done.1), custom_call_target="tpu_custom_call" | custom-call | tf_op jit(solution)/shard_map/factor_modes/pallas_call | solution.py:202
  (14 shorter events, 0.2 us)
Async XLA Ops:
  0.6 2.2 %copy-start = (bf16[8,2048,128]{2,1,0:T(8,128)(2,1)S(1)}, bf16[8,2048,128]{2,1,0:T(8,128)(2,1)}, u32[]{:S(2)}) copy-start(bf16[8,2048,128]{2,1,0:T(8,128)(2,1)} %refs_1_.1) | copy-start | bytes 12582916
  5.8 4.3 %collective-permute-start = (f32[288,128]{1,0:T(8,128)S(1)}, f32[288,128]{1,0:T(8,128)S(1)}, u32[]{:S(2)}, u32[]{:S(2)}) collective-permute-start(f32[288,128]{1,0:T(8,128)S(1)} %constant_dynamic-slice_fusion.3), channel_id=1, source_target_pairs={{0,4},{4,0},{8,12},{12,8},{16,20},{20,16},{24,28},{28,24},{32,36},... | collective-permute-start | bytes 442376 | tf_op jit(solution)/shard_map/ppermute | solution.py:158
  10.2 4.1 %collective-permute-start.1 = (f32[72,128]{1,0:T(8,128)S(1)}, f32[72,128]{1,0:T(8,128)S(1)}, u32[]{:S(2)}, u32[]{:S(2)}) collective-permute-start(f32[72,128]{1,0:T(8,128)S(1)} %get-tuple-element.12), channel_id=1, source_target_pairs={{0,1},{1,2},{2,3},{3,0},{4,5},{5,6},{6,7},{7,4},{8,9},{9,10},{10,1... | collective-permute-start | bytes 110600 | tf_op jit(solution)/shard_map/ppermute | solution.py:164
  10.3 4.0 %collective-permute-start.3 = (f32[72,128]{1,0:T(8,128)S(1)}, f32[72,128]{1,0:T(8,128)S(1)}, u32[]{:S(2)}, u32[]{:S(2)}) collective-permute-start(f32[72,128]{1,0:T(8,128)S(1)} %get-tuple-element.13), channel_id=1, source_target_pairs={{0,3},{1,0},{2,1},{3,2},{4,7},{5,4},{6,5},{7,6},{8,11},{9,8},{10,9... | collective-permute-start | bytes 110600 | tf_op jit(solution)/shard_map/ppermute | solution.py:164
  12.9 4.3 %collective-permute-start.2 = (f32[72,128]{1,0:T(8,128)S(1)}, f32[72,128]{1,0:T(8,128)S(1)}, u32[]{:S(2)}, u32[]{:S(2)}) collective-permute-start(f32[72,128]{1,0:T(8,128)S(1)} %get-tuple-element.14), channel_id=1, source_target_pairs={{0,2},{1,3},{2,0},{3,1},{4,6},{5,7},{6,4},{7,5},{8,10},{9,11},{10,... | collective-permute-start | bytes 110600 | tf_op jit(solution)/shard_map/ppermute | solution.py:164
  17.3 2.9 %collective-permute-start.6 = (f32[72,128]{1,0:T(8,128)S(1)}, f32[72,128]{1,0:T(8,128)S(1)}, u32[]{:S(2)}, u32[]{:S(2)}) collective-permute-start(f32[72,128]{1,0:T(8,128)S(1)} %add_add_fusion.1), channel_id=1, source_target_pairs={{0,24},{4,28},{8,0},{12,4},{16,8},{20,12},{24,16},{28,20},{32,56},... | collective-permute-start | bytes 110600 | tf_op jit(solution)/shard_map/ppermute | solution.py:167
  18.3 4.0 %collective-permute-start.5 = (f32[72,128]{1,0:T(8,128)S(1)}, f32[72,128]{1,0:T(8,128)S(1)}, u32[]{:S(2)}, u32[]{:S(2)}) collective-permute-start(f32[72,128]{1,0:T(8,128)S(1)} %add_add_fusion.1), channel_id=1, source_target_pairs={{0,8},{4,12},{8,16},{12,20},{16,24},{20,28},{24,0},{28,4},{32,40},... | collective-permute-start | bytes 110600 | tf_op jit(solution)/shard_map/ppermute | solution.py:167
  18.8 4.3 %collective-permute-start.4 = (f32[72,128]{1,0:T(8,128)S(1)}, f32[72,128]{1,0:T(8,128)S(1)}, u32[]{:S(2)}, u32[]{:S(2)}) collective-permute-start(f32[72,128]{1,0:T(8,128)S(1)} %add_add_fusion.1), channel_id=1, source_target_pairs={{0,16},{4,20},{8,24},{12,28},{16,0},{20,4},{24,8},{28,12},{32,48},... | collective-permute-start | bytes 110600 | tf_op jit(solution)/shard_map/ppermute | solution.py:167
  23.1 3.2 %collective-permute-start.7 = (f32[72,128]{1,0:T(8,128)S(1)}, f32[72,128]{1,0:T(8,128)S(1)}, u32[]{:S(2)}, u32[]{:S(2)}) collective-permute-start(f32[72,128]{1,0:T(8,128)S(1)} %add_add_fusion), channel_id=1, source_target_pairs={{0,32},{4,36},{8,40},{12,44},{16,48},{20,52},{24,56},{28,60},{32,0... | collective-permute-start | bytes 110600 | tf_op jit(solution)/shard_map/ppermute | solution.py:170
  26.3 3.9 %collective-permute-start.8 = (f32[72,128]{1,0:T(8,128)S(1)}, f32[72,128]{1,0:T(8,128)S(1)}, u32[]{:S(2)}, u32[]{:S(2)}) collective-permute-start(f32[72,128]{1,0:T(8,128)S(1)} %add.90), channel_id=1, source_target_pairs={{0,64},{4,68},{8,72},{12,76},{16,80},{20,84},{24,88},{28,92},{32,9... | collective-permute-start | bytes 110600 | tf_op jit(solution)/shard_map/ppermute | solution.py:170
  30.2 7.5 %collective-permute-start.9 = (f32[72,128]{1,0:T(8,128)S(1)}, f32[72,128]{1,0:T(8,128)S(1)}, u32[]{:S(2)}, u32[]{:S(2)}) collective-permute-start(f32[72,128]{1,0:T(8,128)S(1)} %add.91), channel_id=1, source_target_pairs={{0,128},{4,132},{8,136},{12,140},{16,144},{20,148},{24,152},{28,15... | collective-permute-start | bytes 110600 | tf_op jit(solution)/shard_map/ppermute | solution.py:170
  37.8 2.8 %collective-permute-start.12 = (f32[72,128]{1,0:T(8,128)S(1)}, f32[72,128]{1,0:T(8,128)S(1)}, u32[]{:S(2)}, u32[]{:S(2)}) collective-permute-start(f32[72,128]{1,0:T(8,128)S(1)} %add.92), channel_id=1, source_target_pairs={{0,3},{1,0},{2,1},{3,2},{4,7},{5,4},{6,5},{7,6},{8,11},{9,8},{10,9... | collective-permute-start | bytes 110600 | tf_op jit(solution)/shard_map/ppermute | solution.py:171
  39.0 4.3 %collective-permute-start.11 = (f32[72,128]{1,0:T(8,128)S(1)}, f32[72,128]{1,0:T(8,128)S(1)}, u32[]{:S(2)}, u32[]{:S(2)}) collective-permute-start(f32[72,128]{1,0:T(8,128)S(1)} %add.92), channel_id=1, source_target_pairs={{0,2},{1,3},{2,0},{3,1},{4,6},{5,7},{6,4},{7,5},{8,10},{9,11},{10,... | collective-permute-start | bytes 110600 | tf_op jit(solution)/shard_map/ppermute | solution.py:171
  39.9 4.3 %collective-permute-start.10 = (f32[72,128]{1,0:T(8,128)S(1)}, f32[72,128]{1,0:T(8,128)S(1)}, u32[]{:S(2)}, u32[]{:S(2)}) collective-permute-start(f32[72,128]{1,0:T(8,128)S(1)} %add.92), channel_id=1, source_target_pairs={{0,1},{1,2},{2,3},{3,0},{4,5},{5,6},{6,7},{7,4},{8,9},{9,10},{10,1... | collective-permute-start | bytes 110600 | tf_op jit(solution)/shard_map/ppermute | solution.py:171
  44.3 9.7 %collective-permute-start.13 = (f32[288,128]{1,0:T(8,128)S(1)}, f32[288,128]{1,0:T(8,128)S(1)}, u32[]{:S(2)}, u32[]{:S(2)}) collective-permute-start(f32[288,128]{1,0:T(8,128)S(1)} %pad_maximum_fusion.1), channel_id=1, source_target_pairs={{0,4},{4,0},{8,12},{12,8},{16,20},{20,16},{24,28},{28,24},{32,36},... | collective-permute-start | bytes 442376 | tf_op jit(solution)/shard_map/ppermute | solution.py:183
  54.0 2.2 %copy-start.1 = (bf16[8,2048,128]{2,1,0:T(8,128)(2,1)S(1)}, bf16[8,2048,128]{2,1,0:T(8,128)(2,1)}, u32[]{:S(2)}) copy-start(bf16[8,2048,128]{2,1,0:T(8,128)(2,1)} %refs_1_.1) | copy-start | bytes 12582916

commit v2 on v1

v2 whole, which is shorter than its diff:
```python
import jax
import jax.numpy as jnp
from jax import lax
from jax.experimental import pallas as pl
from jax.experimental.pallas import tpu as pltpu
from jax.sharding import PartitionSpec as P

BLOCK = 8
PANEL = 16
GROUP = 16
LIMIT = 58 * 1024 * 1024


def packing(width):
    groups = width // GROUP
    half = groups // 2
    place = {}
    for a in range(half):
        for r in range(GROUP):
            place[a * GROUP + r] = (a * GROUP + r, 0)
            if a:
                place[(groups - a) * GROUP + r] = (a * GROUP + r, a * GROUP)
    for r in range(GROUP // 2):
        at = half * GROUP + r
        place[at] = (at, 0)
        place[at + GROUP // 2] = (at, width // 2)
    return place, half * GROUP + GROUP // 2


def gram_kernel(planes, width, v_hbm, packed_ref, gram_ref, v_ref, sem):
    def fetch(p):
        return pltpu.make_async_copy(v_hbm.at[p], v_ref.at[p], sem.at[p])

    for p in range(planes):
        fetch(p).start()
    for p in range(planes):
        fetch(p).wait()
        v = v_ref[p]
        gram_ref[pl.ds(p, width, stride=planes), :] = lax.dot_general(
            v, v, (((0,), (0,)), ((), ())), preferred_element_type=jnp.float32
        )
    place, _ = packing(width)
    lanes = lax.broadcasted_iota(jnp.int32, (planes, width), 1)
    for row, (at, roll) in place.items():
        if roll:
            continue
        value = gram_ref[row * planes : (row + 1) * planes, :]
        for other, (other_at, other_roll) in place.items():
            if other_at == at and other_roll:
                moved = pltpu.roll(gram_ref[other * planes : (other + 1) * planes, :], other_roll, 1)
                value = jnp.where(lanes < other_roll, moved, value)
        packed_ref[at * planes : (at + 1) * planes, :] = value


def lane(value, j):
    return jnp.broadcast_to(value[:, j : j + 1], value.shape)


def parts(value):
    high = value.astype(jnp.bfloat16)
    value = value - high.astype(jnp.float32)
    middle = value.astype(jnp.bfloat16)
    return high, middle, (value - middle.astype(jnp.float32)).astype(jnp.bfloat16)


def factor_rows(scale, packed_ref, u_ref, p_ref, x_ref, width, planes):
    place, _ = packing(width)
    lanes = lax.broadcasted_iota(jnp.int32, (planes, width), 1)
    wide = lax.broadcasted_iota(jnp.int32, (width, width), 1)

    def row(ref, i):
        return ref[i * planes : (i + 1) * planes, :]

    for i, (at, roll) in place.items():
        value = row(packed_ref, at)
        x_ref[i * planes : (i + 1) * planes, :] = (pltpu.roll(value, width - roll, 1) if roll else value) * scale

    for first in range(0, width, PANEL):
        last = first + PANEL
        for start in range(first, last, BLOCK):
            kept = (lanes < first) | (lanes >= start)
            inside = (lanes >= start) & (lanes < start + BLOCK)
            rows = [jnp.where(kept, row(x_ref, start + i), 0.0) for i in range(BLOCK)]
            for k in range(first, start):
                source = row(p_ref, k)
                for i in range(BLOCK):
                    rows[i] = rows[i] - lane(source, start + i) * source
                p_ref[k * planes : (k + 1) * planes, :] = jnp.where(inside, 0.0, source)
            cell = {(i, j): lane(rows[i], start + j) for i in range(BLOCK) for j in range(i, BLOCK)}
            for k in range(BLOCK):
                pivot = cell[k, k]
                root = lax.rsqrt(pivot)
                root = root * (1.5 - 0.5 * pivot * root * root)
                for j in range(k + 1, BLOCK):
                    cell[k, j] = cell[k, j] * root
                for i in range(k + 1, BLOCK):
                    for j in range(i, BLOCK):
                        cell[i, j] = cell[i, j] - cell[k, i] * cell[k, j]
                here = lanes == start + k
                whole = rows[k] * root
                u_ref[pl.ds(start + k, planes, stride=width), :] = jnp.where(lanes >= start + k, whole, 0.0)
                whole = jnp.where(here, root, whole)
                p_ref[(start + k) * planes : (start + k + 1) * planes, :] = jnp.where(
                    (lanes <= start + k) | (lanes >= start + BLOCK), whole, 0.0
                )
                for i in range(k + 1, BLOCK):
                    rows[i] = jnp.where(here, 0.0, rows[i]) - cell[k, i] * whole
        if last == width:
            break
        done = (wide[last:, :] >= first) & (wide[last:, :] < last)
        for p in range(planes):
            high, middle, low = parts(p_ref[pl.ds(first * planes + p, PANEL, stride=planes), :])
            change = lax.dot_general(
                jnp.concatenate([high, high, middle, high, low, middle], axis=0),
                jnp.concatenate([high, middle, high, low, high, middle], axis=0),
                (((0,), (0,)), ((), ())),
                preferred_element_type=jnp.float32,
            )
            at = pl.ds(last * planes + p, width - last, stride=planes)
            x_ref[at, :] = jnp.where(done, 0.0, x_ref[at, :]) - change[last:, :]


def modes_kernel(
    scale, planes, width, packed_ref, v_hbm, u_hbm, m_hbm, u_ref, p_ref, x_ref, v_ref, m_ref, in_sem, out_sem, u_sem
):
    def fetch(p):
        return pltpu.make_async_copy(v_hbm.at[p], v_ref.at[p], in_sem.at[p])

    def put(p):
        return pltpu.make_async_copy(m_ref.at[p], m_hbm.at[p], out_sem.at[p])

    for p in range(planes):
        fetch(p).start()
    factor_rows(scale, packed_ref, u_ref, p_ref, x_ref, width, planes)
    put_factor = pltpu.make_async_copy(u_ref, u_hbm, u_sem)
    put_factor.start()
    low_half = lax.broadcasted_iota(jnp.int32, (width, width), 0) >= lax.broadcasted_iota(
        jnp.int32, (width, width), 1
    )
    for p in range(planes):
        high, middle, low = parts(jnp.where(low_half, p_ref[pl.ds(p, width, stride=planes), :], 0.0))
        weights = jnp.concatenate(
            [
                jnp.concatenate([high, middle], axis=1),
                jnp.concatenate([low, jnp.zeros_like(low)], axis=1),
            ],
            axis=0,
        )
        fetch(p).wait()
        v = v_ref[p]
        both = lax.dot_general(
            jnp.concatenate([v, v], axis=1),
            weights,
            (((1,), (1,)), ((), ())),
            preferred_element_type=jnp.float32,
        )
        m_ref[p] = both[:, :width] + both[:, width:]
        put(p).start()
    put_factor.wait()
    for p in range(planes):
        put(p).wait()


def index(z, y, core):
    return (z * 4 + y) * 2 + core


def rows_perm(move):
    return [(index(z, y, c), index(*move(z, y, c))) for z in range(8) for y in range(4) for c in range(2)]


def total(x):
    core = lax.axis_index("rows") % 2
    here = lax.axis_index("batch")
    other_core = rows_perm(lambda z, y, c: (z, y, 1 - c))
    n = x.shape[0] // 2
    x = lax.dynamic_slice_in_dim(x, core * n, n, 0) + lax.ppermute(
        lax.dynamic_slice_in_dim(x, (1 - core) * n, n, 0), "rows", other_core
    )
    m = n // 4
    shift = {d: [(i, (i + d) % 4) for i in range(4)] for d in (1, 2, 3)}
    got = [
        lax.ppermute(lax.dynamic_slice_in_dim(x, ((here + d) % 4) * m, m, 0), "batch", shift[d]) for d in (1, 2, 3)
    ]
    x = lax.dynamic_slice_in_dim(x, here * m, m, 0) + got[0] + got[1] + got[2]
    got = [lax.ppermute(x, "rows", rows_perm(lambda z, y, c: (z, (y + d) % 4, c))) for d in (1, 2, 3)]
    x = (x + got[1]) + (got[0] + got[2])
    for bit in (1, 2, 4):
        x = x + lax.ppermute(x, "rows", rows_perm(lambda z, y, c: (z ^ bit, y, c)))
    got = [x] + [lax.ppermute(x, "batch", shift[d]) for d in (1, 2, 3)]
    x = jnp.concatenate(
        [
            jnp.where(
                here == j,
                got[0],
                jnp.where(here == (j + 1) % 4, got[1], jnp.where(here == (j + 2) % 4, got[2], got[3])),
            )
            for j in range(4)
        ],
        axis=0,
    )
    y = lax.ppermute(x, "rows", other_core)
    return jnp.concatenate([jnp.where(core == 0, x, y), jnp.where(core == 0, y, x)], axis=0)


def shards(velocity):
    planes, rows_dev, width = velocity.shape
    stack = rows_dev * lax.axis_size("rows") * lax.axis_size("batch")
    _, packed_rows = packing(width)
    hbm = pl.BlockSpec(memory_space=pltpu.HBM)
    vmem = pl.BlockSpec(memory_space=pltpu.VMEM)
    packed = pl.pallas_call(
        lambda *refs: gram_kernel(planes, width, *refs),
        in_specs=[hbm],
        out_specs=vmem,
        out_shape=jax.ShapeDtypeStruct((packed_rows * planes, width), jnp.float32),
        scratch_shapes=[
            pltpu.VMEM((width * planes, width), jnp.float32),
            pltpu.VMEM((planes, rows_dev, width), jnp.bfloat16),
            pltpu.SemaphoreType.DMA((planes,)),
        ],
        compiler_params=pltpu.CompilerParams(vmem_limit_bytes=LIMIT),
        name="gram",
    )(velocity)
    packed = total(packed)
    factor, modes = pl.pallas_call(
        lambda *refs: modes_kernel(1.0 / stack, planes, width, *refs),
        in_specs=[vmem, hbm],
        out_specs=[hbm, hbm],
        out_shape=[
            jax.ShapeDtypeStruct((planes * width, width), jnp.float32),
            jax.ShapeDtypeStruct((planes, rows_dev, width), jnp.float32),
        ],
        scratch_shapes=[
            pltpu.VMEM((planes * width, width), jnp.float32),
            pltpu.VMEM((width * planes, width), jnp.float32),
            pltpu.VMEM((width * planes, width), jnp.float32),
            pltpu.VMEM((planes, rows_dev, width), jnp.bfloat16),
            pltpu.VMEM((planes, rows_dev, width), jnp.float32),
            pltpu.SemaphoreType.DMA((planes,)),
            pltpu.SemaphoreType.DMA((planes,)),
            pltpu.SemaphoreType.DMA,
        ],
        compiler_params=pltpu.CompilerParams(vmem_limit_bytes=LIMIT),
        name="factor_modes",
    )(packed, velocity)
    return (factor.reshape(planes, width, width), modes)


def solution(mesh):
    placed = (P(None, "rows", "batch"),)
    return jax.shard_map(
        shards,
        mesh=mesh,
        in_specs=placed,
        out_specs=(P(), P(None, "rows", "batch")),
        check_vma=False,
    )
```

time: 91.4 us -> 70 us (0.77)
  Pallas kernels: 37.8 us -> 18.3 us
  local copies, waits for them, and re-layouts: 4.4 us -> 0.94 us
  other arithmetic: 0.14 us -> 1.75 us
    pallas_call x1, Pallas kernels: 34.9 us -> 13.6 us  [shards(): pl.pallas_call(lambda *refs: modes_kernel(1.0 / stack, planes, width, *re...]
    unnamed x4 -> x0, local copies, waits for them, and re-layouts: 4.37 us -> none
    pallas_call x1, Pallas kernels: 2.91 us -> 4.69 us  [shards(): pl.pallas_call(lambda *refs: gram_kernel(planes, width, *refs), in_specs=...]
where the time goes in v2:
time: 70 us; the launch traced here: 69.9 us
  starting transfers between devices  29.9 us (43%)
  Pallas kernels  18.3 us (26%)
  waiting for transfers between devices  18.1 us (26%)
  other arithmetic  1.75 us (2%)
  local copies, waits for them, and re-layouts  0.94 us (1%)
  between operations  0.88 us (1%)
    pallas_call x1, Pallas kernels, shards(): pl.pallas_call(lambda *refs: modes_kernel(1.0 / stack, planes, width, *re...  13.6 us
    ppermute x3, starting transfers between devices, total(): x = x + lax.ppermute(x, 'rows', rows_perm(lambda z, y, c: (z ^ bit, y, c)))  10.1 us
    ppermute x1, starting transfers between devices, total(): y = lax.ppermute(x, 'rows', other_core)  8.66 us
    pallas_call x1, Pallas kernels, shards(): pl.pallas_call(lambda *refs: gram_kernel(planes, width, *refs), in_specs=...  4.69 us
    ppermute x3, waiting for transfers between devices, total(): x = x + lax.ppermute(x, 'rows', rows_perm(lambda z, y, c: (z ^ bit, y, c)))  4.56 us
    ppermute x3, waiting for transfers between devices, total(): lax.ppermute(lax.dynamic_slice_in_dim(x, (here + d) % 4 * m, m, 0), 'batc...  4.31 us
    ppermute x3, waiting for transfers between devices, total(): got = [x] + [lax.ppermute(x, 'batch', shift[d]) for d in (1, 2, 3)]  4.07 us
    ppermute x1, starting transfers between devices, total(): lax.ppermute(lax.dynamic_slice_in_dim(x, (1 - core) * n, n, 0), 'rows', o...  3.32 us
  transfers between devices with their start and end apart: 14, of which 13 were waited for; matrix products, arithmetic and copies ran while one was open for 0% of the time, Pallas kernels for 0%

profile of v2, /device:TPU:1, one launch (start us, length us, event | category | flops | bytes accessed | tf_op | source)
XLA Modules:
  0.0 69.9 jit_solution(1098102334137384903)
XLA Ops:
  0.6 4.7 %gram.1 = f32[576,128]{1,0:T(8,128)} custom-call(bf16[8,2048,128]{2,1,0:T(8,128)(2,1)} %refs_1_.1), custom_call_target="tpu_custom_call" | custom-call | tf_op jit(solution)/shard_map/gram/pallas_call | solution.py:212
  5.3 0.9 %constant_dynamic-slice_fusion.3 = f32[288,128]{1,0:T(8,128)S(1)} fusion(f32[576,128]{1,0:T(8,128)} %gram.1, s32[]{:T(128)S(6)} %select_n.111), kind=kLoop, calls=%fused_computation.14 | loop fusion | bytes 294916 | tf_op jit(solution)/shard_map/dynamic_slice | solution.py:178
  6.3 3.3 %collective-permute-start = (f32[288,128]{1,0:T(8,128)S(1)}, f32[288,128]{1,0:T(8,128)S(1)}, u32[]{:S(2)}, u32[]{:S(2)}) collective-permute-start(f32[288,128]{1,0:T(8,128)S(1)} %constant_dynamic-slice_fusion.3), channel_id=1, source_target_pairs={{0,4},{4,0},{8,12},{12,8},{16,20},{20,16},{24,28},{28,24},{32,36},... | collective-permute-start | bytes 442376 | tf_op jit(solution)/shard_map/ppermute | solution.py:177
  9.6 1.0 %collective-permute-done = f32[288,128]{1,0:T(8,128)S(1)} collective-permute-done((f32[288,128]{1,0:T(8,128)S(1)}, f32[288,128]{1,0:T(8,128)S(1)}, u32[]{:S(2)}, u32[]{:S(2)}) %collective-permute-start) | collective-permute-done | bytes 147488 | tf_op jit(solution)/shard_map/ppermute | solution.py:177
  10.6 0.9 %dynamic-slice_add_fusion = f32[288,128]{1,0:T(8,128)S(1)} fusion(f32[288,128]{1,0:T(8,128)S(1)} %collective-permute-done, f32[576,128]{1,0:T(8,128)} %gram.1, s32[]{:T(128)S(6)} %select_n.110), kind=kLoop, calls=%fused_computation.2 | loop fusion | flops 36864 | bytes 442372 | tf_op jit(solution)/shard_map/add | solution.py:177
  11.6 0.1 collective-permute-start.1
  11.7 2.7 %collective-permute-start.3 = (f32[72,128]{1,0:T(8,128)S(1)}, f32[72,128]{1,0:T(8,128)S(1)}, u32[]{:S(2)}, u32[]{:S(2)}) collective-permute-start(f32[72,128]{1,0:T(8,128)S(1)} %get-tuple-element.13), channel_id=1, source_target_pairs={{0,3},{1,0},{2,1},{3,2},{4,7},{5,4},{6,5},{7,6},{8,11},{9,8},{10,9... | collective-permute-start | bytes 110600 | tf_op jit(solution)/shard_map/ppermute | solution.py:183
  14.3 1.3 %collective-permute-done.1 = f32[72,128]{1,0:T(8,128)S(1)} collective-permute-done((f32[72,128]{1,0:T(8,128)S(1)}, f32[72,128]{1,0:T(8,128)S(1)}, u32[]{:S(2)}, u32[]{:S(2)}) %collective-permute-start.1) | collective-permute-done | bytes 36896 | tf_op jit(solution)/shard_map/ppermute | solution.py:183
  15.7 0.0 collective-permute-done.3
  15.7 3.0 %collective-permute-done.2 = f32[72,128]{1,0:T(8,128)S(1)} collective-permute-done((f32[72,128]{1,0:T(8,128)S(1)}, f32[72,128]{1,0:T(8,128)S(1)}, u32[]{:S(2)}, u32[]{:S(2)}) %collective-permute-start.2) | collective-permute-done | bytes 36896 | tf_op jit(solution)/shard_map/ppermute | solution.py:183
  18.7 1.1 %collective-permute-start.6 = (f32[72,128]{1,0:T(8,128)S(1)}, f32[72,128]{1,0:T(8,128)S(1)}, u32[]{:S(2)}, u32[]{:S(2)}) collective-permute-start(f32[72,128]{1,0:T(8,128)S(1)} %add_add_fusion.1), channel_id=1, source_target_pairs={{0,24},{4,28},{8,0},{12,4},{16,8},{20,12},{24,16},{28,20},{32,56},... | collective-permute-start | bytes 110600 | tf_op jit(solution)/shard_map/ppermute | solution.py:186
  19.7 0.5 collective-permute-start.5
  20.2 1.2 %collective-permute-start.4 = (f32[72,128]{1,0:T(8,128)S(1)}, f32[72,128]{1,0:T(8,128)S(1)}, u32[]{:S(2)}, u32[]{:S(2)}) collective-permute-start(f32[72,128]{1,0:T(8,128)S(1)} %add_add_fusion.1), channel_id=1, source_target_pairs={{0,16},{4,20},{8,24},{12,28},{16,0},{20,4},{24,8},{28,12},{32,48},... | collective-permute-start | bytes 110600 | tf_op jit(solution)/shard_map/ppermute | solution.py:186
  21.4 0.2 collective-permute-done.6
  21.5 2.2 %collective-permute-done.5 = f32[72,128]{1,0:T(8,128)S(1)} collective-permute-done((f32[72,128]{1,0:T(8,128)S(1)}, f32[72,128]{1,0:T(8,128)S(1)}, u32[]{:S(2)}, u32[]{:S(2)}) %collective-permute-start.5) | collective-permute-done | bytes 36896 | tf_op jit(solution)/shard_map/ppermute | solution.py:186
  23.8 0.8 %collective-permute-done.4 = f32[72,128]{1,0:T(8,128)S(1)} collective-permute-done((f32[72,128]{1,0:T(8,128)S(1)}, f32[72,128]{1,0:T(8,128)S(1)}, u32[]{:S(2)}, u32[]{:S(2)}) %collective-permute-start.4) | collective-permute-done | bytes 36896 | tf_op jit(solution)/shard_map/ppermute | solution.py:186
  24.5 1.4 %collective-permute-start.7 = (f32[72,128]{1,0:T(8,128)S(1)}, f32[72,128]{1,0:T(8,128)S(1)}, u32[]{:S(2)}, u32[]{:S(2)}) collective-permute-start(f32[72,128]{1,0:T(8,128)S(1)} %add_add_fusion), channel_id=1, source_target_pairs={{0,32},{4,36},{8,40},{12,44},{16,48},{20,52},{24,56},{28,60},{32,0... | collective-permute-start | bytes 110600 | tf_op jit(solution)/shard_map/ppermute | solution.py:189
  25.9 1.8 %collective-permute-done.7 = f32[72,128]{1,0:T(8,128)S(1)} collective-permute-done((f32[72,128]{1,0:T(8,128)S(1)}, f32[72,128]{1,0:T(8,128)S(1)}, u32[]{:S(2)}, u32[]{:S(2)}) %collective-permute-start.7) | collective-permute-done | bytes 36896 | tf_op jit(solution)/shard_map/ppermute | solution.py:189
  27.7 2.5 %collective-permute-start.8 = (f32[72,128]{1,0:T(8,128)S(1)}, f32[72,128]{1,0:T(8,128)S(1)}, u32[]{:S(2)}, u32[]{:S(2)}) collective-permute-start(f32[72,128]{1,0:T(8,128)S(1)} %add.90), channel_id=1, source_target_pairs={{0,64},{4,68},{8,72},{12,76},{16,80},{20,84},{24,88},{28,92},{32,9... | collective-permute-start | bytes 110600 | tf_op jit(solution)/shard_map/ppermute | solution.py:189
  30.2 1.4 %collective-permute-done.8 = f32[72,128]{1,0:T(8,128)S(1)} collective-permute-done((f32[72,128]{1,0:T(8,128)S(1)}, f32[72,128]{1,0:T(8,128)S(1)}, u32[]{:S(2)}, u32[]{:S(2)}) %collective-permute-start.8) | collective-permute-done | bytes 36896 | tf_op jit(solution)/shard_map/ppermute | solution.py:189
  31.6 6.2 %collective-permute-start.9 = (f32[72,128]{1,0:T(8,128)S(1)}, f32[72,128]{1,0:T(8,128)S(1)}, u32[]{:S(2)}, u32[]{:S(2)}) collective-permute-start(f32[72,128]{1,0:T(8,128)S(1)} %add.91), channel_id=1, source_target_pairs={{0,128},{4,132},{8,136},{12,140},{16,144},{20,148},{24,152},{28,15... | collective-permute-start | bytes 110600 | tf_op jit(solution)/shard_map/ppermute | solution.py:189
  37.8 1.3 %collective-permute-done.9 = f32[72,128]{1,0:T(8,128)S(1)} collective-permute-done((f32[72,128]{1,0:T(8,128)S(1)}, f32[72,128]{1,0:T(8,128)S(1)}, u32[]{:S(2)}, u32[]{:S(2)}) %collective-permute-start.9) | collective-permute-done | bytes 36896 | tf_op jit(solution)/shard_map/ppermute | solution.py:189
  39.2 1.3 %collective-permute-start.12 = (f32[72,128]{1,0:T(8,128)S(1)}, f32[72,128]{1,0:T(8,128)S(1)}, u32[]{:S(2)}, u32[]{:S(2)}) collective-permute-start(f32[72,128]{1,0:T(8,128)S(1)} %add.92), channel_id=1, source_target_pairs={{0,3},{1,0},{2,1},{3,2},{4,7},{5,4},{6,5},{7,6},{8,11},{9,8},{10,9... | collective-permute-start | bytes 110600 | tf_op jit(solution)/shard_map/ppermute | solution.py:190
  40.4 0.9 %collective-permute-start.11 = (f32[72,128]{1,0:T(8,128)S(1)}, f32[72,128]{1,0:T(8,128)S(1)}, u32[]{:S(2)}, u32[]{:S(2)}) collective-permute-start(f32[72,128]{1,0:T(8,128)S(1)} %add.92), channel_id=1, source_target_pairs={{0,2},{1,3},{2,0},{3,1},{4,6},{5,7},{6,4},{7,5},{8,10},{9,11},{10,... | collective-permute-start | bytes 110600 | tf_op jit(solution)/shard_map/ppermute | solution.py:190
  41.3 0.2 collective-permute-start.10
  41.6 0.4 collective-permute-done.12
  42.0 2.8 %collective-permute-done.11 = f32[72,128]{1,0:T(8,128)S(1)} collective-permute-done((f32[72,128]{1,0:T(8,128)S(1)}, f32[72,128]{1,0:T(8,128)S(1)}, u32[]{:S(2)}, u32[]{:S(2)}) %collective-permute-start.11) | collective-permute-done | bytes 36896 | tf_op jit(solution)/shard_map/ppermute | solution.py:190
  44.7 0.9 %collective-permute-done.10 = f32[72,128]{1,0:T(8,128)S(1)} collective-permute-done((f32[72,128]{1,0:T(8,128)S(1)}, f32[72,128]{1,0:T(8,128)S(1)}, u32[]{:S(2)}, u32[]{:S(2)}) %collective-permute-start.10) | collective-permute-done | bytes 36896 | tf_op jit(solution)/shard_map/ppermute | solution.py:190
  45.7 8.7 %collective-permute-start.13 = (f32[288,128]{1,0:T(8,128)S(1)}, f32[288,128]{1,0:T(8,128)S(1)}, u32[]{:S(2)}, u32[]{:S(2)}) collective-permute-start(f32[288,128]{1,0:T(8,128)S(1)} %pad_maximum_fusion.1), channel_id=1, source_target_pairs={{0,4},{4,0},{8,12},{12,8},{16,20},{20,16},{24,28},{28,24},{32,36},... | collective-permute-start | bytes 442376 | tf_op jit(solution)/shard_map/ppermute | solution.py:202
  54.3 1.0 %collective-permute-done.13 = f32[288,128]{1,0:T(8,128)S(1)} collective-permute-done((f32[288,128]{1,0:T(8,128)S(1)}, f32[288,128]{1,0:T(8,128)S(1)}, u32[]{:S(2)}, u32[]{:S(2)}) %collective-permute-start.13) | collective-permute-done | bytes 147488 | tf_op jit(solution)/shard_map/ppermute | solution.py:202
  55.4 0.7 %pad_maximum_fusion.refs_0_ = f32[576,128]{1,0:T(8,128)} fusion(f32[288,128]{1,0:T(8,128)S(1)} %get-tuple-element.7, f32[288,128]{1,0:T(8,128)S(1)} %get-tuple-element.6), kind=kLoop, calls=%fused_computation | loop fusion | flops 73728 | bytes 589824 | tf_op jit(solution)/shard_map/concatenate | solution.py:203
  56.1 13.6 %factor_modes.1 = (f32[1024,128]{1,0:T(8,128)}, f32[8,2048,128]{2,1,0:T(8,128)}) custom-call(f32[576,128]{1,0:T(8,128)} %pad_maximum_fusion.refs_0_, bf16[8,2048,128]{2,1,0:T(8,128)(2,1)} %refs_1_.1), custom_call_target="tpu_custom_call" | custom-call | tf_op jit(solution)/shard_map/factor_modes/pallas_call | solution.py:226
  (10 shorter events, 0.1 us)
Async XLA Ops:
  6.3 4.3 %collective-permute-start = (f32[288,128]{1,0:T(8,128)S(1)}, f32[288,128]{1,0:T(8,128)S(1)}, u32[]{:S(2)}, u32[]{:S(2)}) collective-permute-start(f32[288,128]{1,0:T(8,128)S(1)} %constant_dynamic-slice_fusion.3), channel_id=1, source_target_pairs={{0,4},{4,0},{8,12},{12,8},{16,20},{20,16},{24,28},{28,24},{32,36},... | collective-permute-start | bytes 442376 | tf_op jit(solution)/shard_map/ppermute | solution.py:177
  11.6 4.1 %collective-permute-start.1 = (f32[72,128]{1,0:T(8,128)S(1)}, f32[72,128]{1,0:T(8,128)S(1)}, u32[]{:S(2)}, u32[]{:S(2)}) collective-permute-start(f32[72,128]{1,0:T(8,128)S(1)} %get-tuple-element.12), channel_id=1, source_target_pairs={{0,1},{1,2},{2,3},{3,0},{4,5},{5,6},{6,7},{7,4},{8,9},{9,10},{10,1... | collective-permute-start | bytes 110600 | tf_op jit(solution)/shard_map/ppermute | solution.py:183
  11.7 4.0 %collective-permute-start.3 = (f32[72,128]{1,0:T(8,128)S(1)}, f32[72,128]{1,0:T(8,128)S(1)}, u32[]{:S(2)}, u32[]{:S(2)}) collective-permute-start(f32[72,128]{1,0:T(8,128)S(1)} %get-tuple-element.13), channel_id=1, source_target_pairs={{0,3},{1,0},{2,1},{3,2},{4,7},{5,4},{6,5},{7,6},{8,11},{9,8},{10,9... | collective-permute-start | bytes 110600 | tf_op jit(solution)/shard_map/ppermute | solution.py:183
  14.3 4.3 %collective-permute-start.2 = (f32[72,128]{1,0:T(8,128)S(1)}, f32[72,128]{1,0:T(8,128)S(1)}, u32[]{:S(2)}, u32[]{:S(2)}) collective-permute-start(f32[72,128]{1,0:T(8,128)S(1)} %get-tuple-element.14), channel_id=1, source_target_pairs={{0,2},{1,3},{2,0},{3,1},{4,6},{5,7},{6,4},{7,5},{8,10},{9,11},{10,... | collective-permute-start | bytes 110600 | tf_op jit(solution)/shard_map/ppermute | solution.py:183
  18.7 2.9 %collective-permute-start.6 = (f32[72,128]{1,0:T(8,128)S(1)}, f32[72,128]{1,0:T(8,128)S(1)}, u32[]{:S(2)}, u32[]{:S(2)}) collective-permute-start(f32[72,128]{1,0:T(8,128)S(1)} %add_add_fusion.1), channel_id=1, source_target_pairs={{0,24},{4,28},{8,0},{12,4},{16,8},{20,12},{24,16},{28,20},{32,56},... | collective-permute-start | bytes 110600 | tf_op jit(solution)/shard_map/ppermute | solution.py:186
  19.7 4.0 %collective-permute-start.5 = (f32[72,128]{1,0:T(8,128)S(1)}, f32[72,128]{1,0:T(8,128)S(1)}, u32[]{:S(2)}, u32[]{:S(2)}) collective-permute-start(f32[72,128]{1,0:T(8,128)S(1)} %add_add_fusion.1), channel_id=1, source_target_pairs={{0,8},{4,12},{8,16},{12,20},{16,24},{20,28},{24,0},{28,4},{32,40},... | collective-permute-start | bytes 110600 | tf_op jit(solution)/shard_map/ppermute | solution.py:186
  20.2 4.3 %collective-permute-start.4 = (f32[72,128]{1,0:T(8,128)S(1)}, f32[72,128]{1,0:T(8,128)S(1)}, u32[]{:S(2)}, u32[]{:S(2)}) collective-permute-start(f32[72,128]{1,0:T(8,128)S(1)} %add_add_fusion.1), channel_id=1, source_target_pairs={{0,16},{4,20},{8,24},{12,28},{16,0},{20,4},{24,8},{28,12},{32,48},... | collective-permute-start | bytes 110600 | tf_op jit(solution)/shard_map/ppermute | solution.py:186
  24.5 3.2 %collective-permute-start.7 = (f32[72,128]{1,0:T(8,128)S(1)}, f32[72,128]{1,0:T(8,128)S(1)}, u32[]{:S(2)}, u32[]{:S(2)}) collective-permute-start(f32[72,128]{1,0:T(8,128)S(1)} %add_add_fusion), channel_id=1, source_target_pairs={{0,32},{4,36},{8,40},{12,44},{16,48},{20,52},{24,56},{28,60},{32,0... | collective-permute-start | bytes 110600 | tf_op jit(solution)/shard_map/ppermute | solution.py:189
  27.7 3.9 %collective-permute-start.8 = (f32[72,128]{1,0:T(8,128)S(1)}, f32[72,128]{1,0:T(8,128)S(1)}, u32[]{:S(2)}, u32[]{:S(2)}) collective-permute-start(f32[72,128]{1,0:T(8,128)S(1)} %add.90), channel_id=1, source_target_pairs={{0,64},{4,68},{8,72},{12,76},{16,80},{20,84},{24,88},{28,92},{32,9... | collective-permute-start | bytes 110600 | tf_op jit(solution)/shard_map/ppermute | solution.py:189
  31.6 7.5 %collective-permute-start.9 = (f32[72,128]{1,0:T(8,128)S(1)}, f32[72,128]{1,0:T(8,128)S(1)}, u32[]{:S(2)}, u32[]{:S(2)}) collective-permute-start(f32[72,128]{1,0:T(8,128)S(1)} %add.91), channel_id=1, source_target_pairs={{0,128},{4,132},{8,136},{12,140},{16,144},{20,148},{24,152},{28,15... | collective-permute-start | bytes 110600 | tf_op jit(solution)/shard_map/ppermute | solution.py:189
  39.2 2.8 %collective-permute-start.12 = (f32[72,128]{1,0:T(8,128)S(1)}, f32[72,128]{1,0:T(8,128)S(1)}, u32[]{:S(2)}, u32[]{:S(2)}) collective-permute-start(f32[72,128]{1,0:T(8,128)S(1)} %add.92), channel_id=1, source_target_pairs={{0,3},{1,0},{2,1},{3,2},{4,7},{5,4},{6,5},{7,6},{8,11},{9,8},{10,9... | collective-permute-start | bytes 110600 | tf_op jit(solution)/shard_map/ppermute | solution.py:190
  40.4 4.3 %collective-permute-start.11 = (f32[72,128]{1,0:T(8,128)S(1)}, f32[72,128]{1,0:T(8,128)S(1)}, u32[]{:S(2)}, u32[]{:S(2)}) collective-permute-start(f32[72,128]{1,0:T(8,128)S(1)} %add.92), channel_id=1, source_target_pairs={{0,2},{1,3},{2,0},{3,1},{4,6},{5,7},{6,4},{7,5},{8,10},{9,11},{10,... | collective-permute-start | bytes 110600 | tf_op jit(solution)/shard_map/ppermute | solution.py:190
  41.3 4.3 %collective-permute-start.10 = (f32[72,128]{1,0:T(8,128)S(1)}, f32[72,128]{1,0:T(8,128)S(1)}, u32[]{:S(2)}, u32[]{:S(2)}) collective-permute-start(f32[72,128]{1,0:T(8,128)S(1)} %add.92), channel_id=1, source_target_pairs={{0,1},{1,2},{2,3},{3,0},{4,5},{5,6},{6,7},{7,4},{8,9},{9,10},{10,1... | collective-permute-start | bytes 110600 | tf_op jit(solution)/shard_map/ppermute | solution.py:190
  45.7 9.7 %collective-permute-start.13 = (f32[288,128]{1,0:T(8,128)S(1)}, f32[288,128]{1,0:T(8,128)S(1)}, u32[]{:S(2)}, u32[]{:S(2)}) collective-permute-start(f32[288,128]{1,0:T(8,128)S(1)} %pad_maximum_fusion.1), channel_id=1, source_target_pairs={{0,4},{4,0},{8,12},{12,8},{16,20},{20,16},{24,28},{28,24},{32,36},... | collective-permute-start | bytes 442376 | tf_op jit(solution)/shard_map/ppermute | solution.py:202

commit v3 on v2

--- a/solution.py
+++ b/solution.py
@@ -8,7 +8,7 @@
 BLOCK = 8
 PANEL = 16
 GROUP = 16
-LIMIT = 58 * 1024 * 1024
+LIMIT = 51 * 1024 * 1024
 
 
 def packing(width):
@@ -161,45 +161,37 @@
         put(p).wait()
 
 
-def index(z, y, core):
-    return (z * 4 + y) * 2 + core
-
-
-def rows_perm(move):
-    return [(index(z, y, c), index(*move(z, y, c))) for z in range(8) for y in range(4) for c in range(2)]
+def flip(x, axis, mask):
+    step = {"z": 8, "y": 2, "core": 1}
+    if axis == "x":
+        return lax.ppermute(x, "batch", [(i, i ^ mask) for i in range(lax.axis_size("batch"))])
+    return lax.ppermute(x, "rows", [(i, i ^ (mask * step[axis])) for i in range(lax.axis_size("rows"))])
 
 
 def total(x):
     core = lax.axis_index("rows") % 2
     here = lax.axis_index("batch")
-    other_core = rows_perm(lambda z, y, c: (z, y, 1 - c))
-    n = x.shape[0] // 2
-    x = lax.dynamic_slice_in_dim(x, core * n, n, 0) + lax.ppermute(
-        lax.dynamic_slice_in_dim(x, (1 - core) * n, n, 0), "rows", other_core
-    )
-    m = n // 4
-    shift = {d: [(i, (i + d) % 4) for i in range(4)] for d in (1, 2, 3)}
-    got = [
-        lax.ppermute(lax.dynamic_slice_in_dim(x, ((here + d) % 4) * m, m, 0), "batch", shift[d]) for d in (1, 2, 3)
-    ]
-    x = lax.dynamic_slice_in_dim(x, here * m, m, 0) + got[0] + got[1] + got[2]
-    got = [lax.ppermute(x, "rows", rows_perm(lambda z, y, c: (z, (y + d) % 4, c))) for d in (1, 2, 3)]
+    half = x.shape[0] // 2
+    x = lax.dynamic_slice_in_dim(x, core * half, half, 0) + flip(
+        lax.dynamic_slice_in_dim(x, (1 - core) * half, half, 0), "core", 1
+    )
+    part = half // 4
+    got = [flip(lax.dynamic_slice_in_dim(x, (here ^ d) * part, part, 0), "x", d) for d in (1, 2, 3)]
+    x = (lax.dynamic_slice_in_dim(x, here * part, part, 0) + got[1]) + (got[0] + got[2])
+    x = x + flip(x, "y", 1)
+    x = x + flip(x, "y", 3)
+    x = x + flip(x, "z", 7)
+    got = [flip(x, "z", d) for d in (1, 2, 3)]
     x = (x + got[1]) + (got[0] + got[2])
-    for bit in (1, 2, 4):
-        x = x + lax.ppermute(x, "rows", rows_perm(lambda z, y, c: (z ^ bit, y, c)))
-    got = [x] + [lax.ppermute(x, "batch", shift[d]) for d in (1, 2, 3)]
+    got = [x] + [flip(x, "x", d) for d in (1, 2, 3)]
     x = jnp.concatenate(
         [
-            jnp.where(
-                here == j,
-                got[0],
-                jnp.where(here == (j + 1) % 4, got[1], jnp.where(here == (j + 2) % 4, got[2], got[3])),
-            )
+            jnp.where(here == j, got[0], jnp.where(here == j ^ 1, got[1], jnp.where(here == j ^ 2, got[2], got[3])))
             for j in range(4)
         ],
         axis=0,
     )
-    y = lax.ppermute(x, "rows", other_core)
+    y = flip(x, "core", 1)
     return jnp.concatenate([jnp.where(core == 0, x, y), jnp.where(core == 0, y, x)], axis=0)
 
 

time: 70 us -> 63.3 us (0.904)
  waiting for transfers between devices: 18.1 us -> 15.1 us
  other arithmetic: 1.75 us -> 0.14 us
  Pallas kernels: 18.3 us -> 17.2 us
  local copies, waits for them, and re-layouts: 0.94 us -> 0.04 us
    ppermute x14, waiting for transfers between devices: 18.1 us -> 15.1 us  [the longest x8 9.51 us: flip(): lax.ppermute(x, 'rows', [(i, i ^ mask * step[axis]) for i in range(lax.ax...]
    add x5, other arithmetic: 0.96 us -> 0.05 us  [the longest x1 0.02 us: total(): lax.dynamic_slice_in_dim(x, core * half, half, 0)]
    dynamic_slice x2, local copies, waits for them, and re-layouts: 0.94 us -> 0.04 us  [the longest x1 0.02 us: total(): lax.dynamic_slice_in_dim(x, (here ^ d) * part, part, 0)]
    pallas_call x1, Pallas kernels: 4.69 us -> 3.98 us  [shards(): pl.pallas_call(lambda *refs: gram_kernel(planes, width, *refs), in_specs=...]
    concatenate x1, other arithmetic: 0.73 us -> 0.02 us  [total(): jnp.concatenate([jnp.where(core == 0, x, y), jnp.where(core == 0, y, x)],...]
  transfers between devices with their start and end apart: 14 -> 14, of which waited for: 13 -> 12; matrix products, arithmetic and copies ran while one was open for 0% -> 0% of each run, Pallas kernels for 0% -> 0%
where the time goes in v3:
time: 63.3 us; the launch traced here: 63.2 us
  starting transfers between devices  29.8 us (47%)
  Pallas kernels  17.2 us (27%)
  waiting for transfers between devices  15.1 us (24%)
  between operations  0.89 us (1%)
    ppermute x8, starting transfers between devices, flip(): lax.ppermute(x, 'rows', [(i, i ^ mask * step[axis]) for i in range(lax.ax...  23.8 us
    pallas_call x1, Pallas kernels, shards(): pl.pallas_call(lambda *refs: modes_kernel(1.0 / stack, planes, width, *re...  13.2 us
    ppermute x8, waiting for transfers between devices, flip(): lax.ppermute(x, 'rows', [(i, i ^ mask * step[axis]) for i in range(lax.ax...  9.51 us
    ppermute x6, starting transfers between devices, flip(): lax.ppermute(x, 'batch', [(i, i ^ mask) for i in range(lax.axis_size('bat...  6.08 us
    ppermute x6, waiting for transfers between devices, flip(): lax.ppermute(x, 'batch', [(i, i ^ mask) for i in range(lax.axis_size('bat...  5.61 us
    pallas_call x1, Pallas kernels, shards(): pl.pallas_call(lambda *refs: gram_kernel(planes, width, *refs), in_specs=...  3.98 us
  transfers between devices with their start and end apart: 14, of which 12 were waited for; matrix products, arithmetic and copies ran while one was open for 0% of the time, Pallas kernels for 0%

profile of v3, /device:TPU:1, one launch (start us, length us, event | category | flops | bytes accessed | tf_op | source)
XLA Modules:
  0.0 63.2 jit_solution(12237636132785354467)
XLA Ops:
  0.6 4.0 %gram.1 = f32[576,128]{1,0:T(8,128)S(1)} custom-call(bf16[8,2048,128]{2,1,0:T(8,128)(2,1)} %refs_1_.1), custom_call_target="tpu_custom_call" | custom-call | tf_op jit(solution)/shard_map/gram/pallas_call | solution.py:204
  4.7 3.3 %collective-permute-start = (f32[288,128]{1,0:T(8,128)S(1)}, f32[288,128]{1,0:T(8,128)S(1)}, u32[]{:S(2)}, u32[]{:S(2)}) collective-permute-start(f32[288,128]{1,0:T(8,128)S(1)} %constant_dynamic-slice_fusion.3), channel_id=1, source_target_pairs={{0,4},{4,0},{8,12},{12,8},{16,20},{20,16},{24,28},{28,24},{32,36},... | collective-permute-start | bytes 442376 | tf_op jit(solution)/shard_map/ppermute | solution.py:168
  8.0 1.0 %collective-permute-done = f32[288,128]{1,0:T(8,128)S(1)} collective-permute-done((f32[288,128]{1,0:T(8,128)S(1)}, f32[288,128]{1,0:T(8,128)S(1)}, u32[]{:S(2)}, u32[]{:S(2)}) %collective-permute-start) | collective-permute-done | bytes 147488 | tf_op jit(solution)/shard_map/ppermute | solution.py:168
  9.0 1.1 %collective-permute-start.1 = (f32[72,128]{1,0:T(8,128)S(1)}, f32[72,128]{1,0:T(8,128)S(1)}, u32[]{:S(2)}, u32[]{:S(2)}) collective-permute-start(f32[72,128]{1,0:T(8,128)S(1)} %get-tuple-element.12), channel_id=1, source_target_pairs={{0,2},{1,3},{2,0},{3,1},{4,6},{5,7},{6,4},{7,5},{8,10},{9,11},{10,... | collective-permute-start | bytes 110600 | tf_op jit(solution)/shard_map/ppermute | solution.py:167
  10.1 0.9 %collective-permute-start.3 = (f32[72,128]{1,0:T(8,128)S(1)}, f32[72,128]{1,0:T(8,128)S(1)}, u32[]{:S(2)}, u32[]{:S(2)}) collective-permute-start(f32[72,128]{1,0:T(8,128)S(1)} %get-tuple-element.13), channel_id=1, source_target_pairs={{0,3},{1,2},{2,1},{3,0},{4,7},{5,6},{6,5},{7,4},{8,11},{9,10},{10,... | collective-permute-start | bytes 110600 | tf_op jit(solution)/shard_map/ppermute | solution.py:167
  11.0 0.8 %collective-permute-start.2 = (f32[72,128]{1,0:T(8,128)S(1)}, f32[72,128]{1,0:T(8,128)S(1)}, u32[]{:S(2)}, u32[]{:S(2)}) collective-permute-start(f32[72,128]{1,0:T(8,128)S(1)} %get-tuple-element.14), channel_id=1, source_target_pairs={{0,1},{1,0},{2,3},{3,2},{4,5},{5,4},{6,7},{7,6},{8,9},{9,8},{10,11... | collective-permute-start | bytes 110600 | tf_op jit(solution)/shard_map/ppermute | solution.py:167
  11.8 1.7 %collective-permute-done.1 = f32[72,128]{1,0:T(8,128)S(1)} collective-permute-done((f32[72,128]{1,0:T(8,128)S(1)}, f32[72,128]{1,0:T(8,128)S(1)}, u32[]{:S(2)}, u32[]{:S(2)}) %collective-permute-start.1) | collective-permute-done | bytes 36896 | tf_op jit(solution)/shard_map/ppermute | solution.py:167
  13.4 1.1 %collective-permute-done.3 = f32[72,128]{1,0:T(8,128)S(1)} collective-permute-done((f32[72,128]{1,0:T(8,128)S(1)}, f32[72,128]{1,0:T(8,128)S(1)}, u32[]{:S(2)}, u32[]{:S(2)}) %collective-permute-start.3) | collective-permute-done | bytes 36896 | tf_op jit(solution)/shard_map/ppermute | solution.py:167
  14.6 0.0 collective-permute-done.2
  14.6 1.0 %collective-permute-start.4 = (f32[72,128]{1,0:T(8,128)S(1)}, f32[72,128]{1,0:T(8,128)S(1)}, u32[]{:S(2)}, u32[]{:S(2)}) collective-permute-start(f32[72,128]{1,0:T(8,128)S(1)} %add_add_fusion.1), channel_id=1, source_target_pairs={{0,8},{4,12},{8,0},{12,4},{16,24},{20,28},{24,16},{28,20},{32,40},... | collective-permute-start | bytes 110600 | tf_op jit(solution)/shard_map/ppermute | solution.py:168
  15.6 1.9 %collective-permute-done.4 = f32[72,128]{1,0:T(8,128)S(1)} collective-permute-done((f32[72,128]{1,0:T(8,128)S(1)}, f32[72,128]{1,0:T(8,128)S(1)}, u32[]{:S(2)}, u32[]{:S(2)}) %collective-permute-start.4) | collective-permute-done | bytes 36896 | tf_op jit(solution)/shard_map/ppermute | solution.py:168
  17.5 2.3 %collective-permute-start.5 = (f32[72,128]{1,0:T(8,128)S(1)}, f32[72,128]{1,0:T(8,128)S(1)}, u32[]{:S(2)}, u32[]{:S(2)}) collective-permute-start(f32[72,128]{1,0:T(8,128)S(1)} %add.63), channel_id=1, source_target_pairs={{0,24},{4,28},{8,16},{12,20},{16,8},{20,12},{24,0},{28,4},{32,56},... | collective-permute-start | bytes 110600 | tf_op jit(solution)/shard_map/ppermute | solution.py:168
  19.8 1.7 %collective-permute-done.5 = f32[72,128]{1,0:T(8,128)S(1)} collective-permute-done((f32[72,128]{1,0:T(8,128)S(1)}, f32[72,128]{1,0:T(8,128)S(1)}, u32[]{:S(2)}, u32[]{:S(2)}) %collective-permute-start.5) | collective-permute-done | bytes 36896 | tf_op jit(solution)/shard_map/ppermute | solution.py:168
  21.5 5.2 %collective-permute-start.6 = (f32[72,128]{1,0:T(8,128)S(1)}, f32[72,128]{1,0:T(8,128)S(1)}, u32[]{:S(2)}, u32[]{:S(2)}) collective-permute-start(f32[72,128]{1,0:T(8,128)S(1)} %add.64), channel_id=1, source_target_pairs={{0,224},{4,228},{8,232},{12,236},{16,240},{20,244},{24,248},{28,25... | collective-permute-start | bytes 110600 | tf_op jit(solution)/shard_map/ppermute | solution.py:168
  26.7 1.3 %collective-permute-done.6 = f32[72,128]{1,0:T(8,128)S(1)} collective-permute-done((f32[72,128]{1,0:T(8,128)S(1)}, f32[72,128]{1,0:T(8,128)S(1)}, u32[]{:S(2)}, u32[]{:S(2)}) %collective-permute-start.6) | collective-permute-done | bytes 36896 | tf_op jit(solution)/shard_map/ppermute | solution.py:168
  28.1 1.6 %collective-permute-start.9 = (f32[72,128]{1,0:T(8,128)S(1)}, f32[72,128]{1,0:T(8,128)S(1)}, u32[]{:S(2)}, u32[]{:S(2)}) collective-permute-start(f32[72,128]{1,0:T(8,128)S(1)} %add.65), channel_id=1, source_target_pairs={{0,96},{4,100},{8,104},{12,108},{16,112},{20,116},{24,120},{28,124... | collective-permute-start | bytes 110600 | tf_op jit(solution)/shard_map/ppermute | solution.py:168
  29.7 0.7 %collective-permute-start.8 = (f32[72,128]{1,0:T(8,128)S(1)}, f32[72,128]{1,0:T(8,128)S(1)}, u32[]{:S(2)}, u32[]{:S(2)}) collective-permute-start(f32[72,128]{1,0:T(8,128)S(1)} %add.65), channel_id=1, source_target_pairs={{0,32},{4,36},{8,40},{12,44},{16,48},{20,52},{24,56},{28,60},{32,0... | collective-permute-start | bytes 110600 | tf_op jit(solution)/shard_map/ppermute | solution.py:168
  30.5 1.2 %collective-permute-start.7 = (f32[72,128]{1,0:T(8,128)S(1)}, f32[72,128]{1,0:T(8,128)S(1)}, u32[]{:S(2)}, u32[]{:S(2)}) collective-permute-start(f32[72,128]{1,0:T(8,128)S(1)} %add.65), channel_id=1, source_target_pairs={{0,64},{4,68},{8,72},{12,76},{16,80},{20,84},{24,88},{28,92},{32,9... | collective-permute-start | bytes 110600 | tf_op jit(solution)/shard_map/ppermute | solution.py:168
  31.6 1.2 %collective-permute-done.9 = f32[72,128]{1,0:T(8,128)S(1)} collective-permute-done((f32[72,128]{1,0:T(8,128)S(1)}, f32[72,128]{1,0:T(8,128)S(1)}, u32[]{:S(2)}, u32[]{:S(2)}) %collective-permute-start.9) | collective-permute-done | bytes 36896 | tf_op jit(solution)/shard_map/ppermute | solution.py:168
  32.8 0.1 collective-permute-done.8
  32.9 1.3 %collective-permute-done.7 = f32[72,128]{1,0:T(8,128)S(1)} collective-permute-done((f32[72,128]{1,0:T(8,128)S(1)}, f32[72,128]{1,0:T(8,128)S(1)}, u32[]{:S(2)}, u32[]{:S(2)}) %collective-permute-start.7) | collective-permute-done | bytes 36896 | tf_op jit(solution)/shard_map/ppermute | solution.py:168
  34.2 1.8 %collective-permute-start.12 = (f32[72,128]{1,0:T(8,128)S(1)}, f32[72,128]{1,0:T(8,128)S(1)}, u32[]{:S(2)}, u32[]{:S(2)}) collective-permute-start(f32[72,128]{1,0:T(8,128)S(1)} %add_add_fusion), channel_id=1, source_target_pairs={{0,3},{1,2},{2,1},{3,0},{4,7},{5,6},{6,5},{7,4},{8,11},{9,10},{10,... | collective-permute-start | bytes 110600 | tf_op jit(solution)/shard_map/ppermute | solution.py:167
  36.1 0.3 collective-permute-start.11
  36.4 1.2 %collective-permute-start.10 = (f32[72,128]{1,0:T(8,128)S(1)}, f32[72,128]{1,0:T(8,128)S(1)}, u32[]{:S(2)}, u32[]{:S(2)}) collective-permute-start(f32[72,128]{1,0:T(8,128)S(1)} %add_add_fusion), channel_id=1, source_target_pairs={{0,1},{1,0},{2,3},{3,2},{4,5},{5,4},{6,7},{7,6},{8,9},{9,8},{10,11... | collective-permute-start | bytes 110600 | tf_op jit(solution)/shard_map/ppermute | solution.py:167
  37.6 0.8 %collective-permute-done.12 = f32[72,128]{1,0:T(8,128)S(1)} collective-permute-done((f32[72,128]{1,0:T(8,128)S(1)}, f32[72,128]{1,0:T(8,128)S(1)}, u32[]{:S(2)}, u32[]{:S(2)}) %collective-permute-start.12) | collective-permute-done | bytes 36896 | tf_op jit(solution)/shard_map/ppermute | solution.py:167
  38.4 2.0 %collective-permute-done.11 = f32[72,128]{1,0:T(8,128)S(1)} collective-permute-done((f32[72,128]{1,0:T(8,128)S(1)}, f32[72,128]{1,0:T(8,128)S(1)}, u32[]{:S(2)}, u32[]{:S(2)}) %collective-permute-start.11) | collective-permute-done | bytes 36896 | tf_op jit(solution)/shard_map/ppermute | solution.py:167
  40.4 0.0 collective-permute-done.10
  40.4 8.3 %collective-permute-start.13 = (f32[288,128]{1,0:T(8,128)S(1)}, f32[288,128]{1,0:T(8,128)S(1)}, u32[]{:S(2)}, u32[]{:S(2)}) collective-permute-start(f32[288,128]{1,0:T(8,128)S(1)} %pad_maximum_fusion.1), channel_id=1, source_target_pairs={{0,4},{4,0},{8,12},{12,8},{16,20},{20,16},{24,28},{28,24},{32,36},... | collective-permute-start | bytes 442376 | tf_op jit(solution)/shard_map/ppermute | solution.py:168
  48.8 1.0 %collective-permute-done.13 = f32[288,128]{1,0:T(8,128)S(1)} collective-permute-done((f32[288,128]{1,0:T(8,128)S(1)}, f32[288,128]{1,0:T(8,128)S(1)}, u32[]{:S(2)}, u32[]{:S(2)}) %collective-permute-start.13) | collective-permute-done | bytes 147488 | tf_op jit(solution)/shard_map/ppermute | solution.py:168
  49.8 13.2 %factor_modes.1 = (f32[1024,128]{1,0:T(8,128)}, f32[8,2048,128]{2,1,0:T(8,128)}) custom-call(f32[576,128]{1,0:T(8,128)S(1)} %pad_maximum_fusion.refs_0_, bf16[8,2048,128]{2,1,0:T(8,128)(2,1)} %refs_1_.1), custom_call_target="tpu_custom_call" | custom-call | tf_op jit(solution)/shard_map/factor_modes/pallas_call | solution.py:218
  (12 shorter events, 0.2 us)
Async XLA Ops:
  4.7 4.3 %collective-permute-start = (f32[288,128]{1,0:T(8,128)S(1)}, f32[288,128]{1,0:T(8,128)S(1)}, u32[]{:S(2)}, u32[]{:S(2)}) collective-permute-start(f32[288,128]{1,0:T(8,128)S(1)} %constant_dynamic-slice_fusion.3), channel_id=1, source_target_pairs={{0,4},{4,0},{8,12},{12,8},{16,20},{20,16},{24,28},{28,24},{32,36},... | collective-permute-start | bytes 442376 | tf_op jit(solution)/shard_map/ppermute | solution.py:168
  9.0 4.4 %collective-permute-start.1 = (f32[72,128]{1,0:T(8,128)S(1)}, f32[72,128]{1,0:T(8,128)S(1)}, u32[]{:S(2)}, u32[]{:S(2)}) collective-permute-start(f32[72,128]{1,0:T(8,128)S(1)} %get-tuple-element.12), channel_id=1, source_target_pairs={{0,2},{1,3},{2,0},{3,1},{4,6},{5,7},{6,4},{7,5},{8,10},{9,11},{10,... | collective-permute-start | bytes 110600 | tf_op jit(solution)/shard_map/ppermute | solution.py:167
  10.1 4.4 %collective-permute-start.3 = (f32[72,128]{1,0:T(8,128)S(1)}, f32[72,128]{1,0:T(8,128)S(1)}, u32[]{:S(2)}, u32[]{:S(2)}) collective-permute-start(f32[72,128]{1,0:T(8,128)S(1)} %get-tuple-element.13), channel_id=1, source_target_pairs={{0,3},{1,2},{2,1},{3,0},{4,7},{5,6},{6,5},{7,4},{8,11},{9,10},{10,... | collective-permute-start | bytes 110600 | tf_op jit(solution)/shard_map/ppermute | solution.py:167
  11.0 3.6 %collective-permute-start.2 = (f32[72,128]{1,0:T(8,128)S(1)}, f32[72,128]{1,0:T(8,128)S(1)}, u32[]{:S(2)}, u32[]{:S(2)}) collective-permute-start(f32[72,128]{1,0:T(8,128)S(1)} %get-tuple-element.14), channel_id=1, source_target_pairs={{0,1},{1,0},{2,3},{3,2},{4,5},{5,4},{6,7},{7,6},{8,9},{9,8},{10,11... | collective-permute-start | bytes 110600 | tf_op jit(solution)/shard_map/ppermute | solution.py:167
  14.6 2.9 %collective-permute-start.4 = (f32[72,128]{1,0:T(8,128)S(1)}, f32[72,128]{1,0:T(8,128)S(1)}, u32[]{:S(2)}, u32[]{:S(2)}) collective-permute-start(f32[72,128]{1,0:T(8,128)S(1)} %add_add_fusion.1), channel_id=1, source_target_pairs={{0,8},{4,12},{8,0},{12,4},{16,24},{20,28},{24,16},{28,20},{32,40},... | collective-permute-start | bytes 110600 | tf_op jit(solution)/shard_map/ppermute | solution.py:168
  17.5 4.0 %collective-permute-start.5 = (f32[72,128]{1,0:T(8,128)S(1)}, f32[72,128]{1,0:T(8,128)S(1)}, u32[]{:S(2)}, u32[]{:S(2)}) collective-permute-start(f32[72,128]{1,0:T(8,128)S(1)} %add.63), channel_id=1, source_target_pairs={{0,24},{4,28},{8,16},{12,20},{16,8},{20,12},{24,0},{28,4},{32,56},... | collective-permute-start | bytes 110600 | tf_op jit(solution)/shard_map/ppermute | solution.py:168
  21.5 6.6 %collective-permute-start.6 = (f32[72,128]{1,0:T(8,128)S(1)}, f32[72,128]{1,0:T(8,128)S(1)}, u32[]{:S(2)}, u32[]{:S(2)}) collective-permute-start(f32[72,128]{1,0:T(8,128)S(1)} %add.64), channel_id=1, source_target_pairs={{0,224},{4,228},{8,232},{12,236},{16,240},{20,244},{24,248},{28,25... | collective-permute-start | bytes 110600 | tf_op jit(solution)/shard_map/ppermute | solution.py:168
  28.1 4.7 %collective-permute-start.9 = (f32[72,128]{1,0:T(8,128)S(1)}, f32[72,128]{1,0:T(8,128)S(1)}, u32[]{:S(2)}, u32[]{:S(2)}) collective-permute-start(f32[72,128]{1,0:T(8,128)S(1)} %add.65), channel_id=1, source_target_pairs={{0,96},{4,100},{8,104},{12,108},{16,112},{20,116},{24,120},{28,124... | collective-permute-start | bytes 110600 | tf_op jit(solution)/shard_map/ppermute | solution.py:168
  29.7 3.2 %collective-permute-start.8 = (f32[72,128]{1,0:T(8,128)S(1)}, f32[72,128]{1,0:T(8,128)S(1)}, u32[]{:S(2)}, u32[]{:S(2)}) collective-permute-start(f32[72,128]{1,0:T(8,128)S(1)} %add.65), channel_id=1, source_target_pairs={{0,32},{4,36},{8,40},{12,44},{16,48},{20,52},{24,56},{28,60},{32,0... | collective-permute-start | bytes 110600 | tf_op jit(solution)/shard_map/ppermute | solution.py:168
  30.5 3.7 %collective-permute-start.7 = (f32[72,128]{1,0:T(8,128)S(1)}, f32[72,128]{1,0:T(8,128)S(1)}, u32[]{:S(2)}, u32[]{:S(2)}) collective-permute-start(f32[72,128]{1,0:T(8,128)S(1)} %add.65), channel_id=1, source_target_pairs={{0,64},{4,68},{8,72},{12,76},{16,80},{20,84},{24,88},{28,92},{32,9... | collective-permute-start | bytes 110600 | tf_op jit(solution)/shard_map/ppermute | solution.py:168
  34.2 4.1 %collective-permute-start.12 = (f32[72,128]{1,0:T(8,128)S(1)}, f32[72,128]{1,0:T(8,128)S(1)}, u32[]{:S(2)}, u32[]{:S(2)}) collective-permute-start(f32[72,128]{1,0:T(8,128)S(1)} %add_add_fusion), channel_id=1, source_target_pairs={{0,3},{1,2},{2,1},{3,0},{4,7},{5,6},{6,5},{7,4},{8,11},{9,10},{10,... | collective-permute-start | bytes 110600 | tf_op jit(solution)/shard_map/ppermute | solution.py:167
  36.1 4.3 %collective-permute-start.11 = (f32[72,128]{1,0:T(8,128)S(1)}, f32[72,128]{1,0:T(8,128)S(1)}, u32[]{:S(2)}, u32[]{:S(2)}) collective-permute-start(f32[72,128]{1,0:T(8,128)S(1)} %add_add_fusion), channel_id=1, source_target_pairs={{0,2},{1,3},{2,0},{3,1},{4,6},{5,7},{6,4},{7,5},{8,10},{9,11},{10,... | collective-permute-start | bytes 110600 | tf_op jit(solution)/shard_map/ppermute | solution.py:167
  36.4 4.0 %collective-permute-start.10 = (f32[72,128]{1,0:T(8,128)S(1)}, f32[72,128]{1,0:T(8,128)S(1)}, u32[]{:S(2)}, u32[]{:S(2)}) collective-permute-start(f32[72,128]{1,0:T(8,128)S(1)} %add_add_fusion), channel_id=1, source_target_pairs={{0,1},{1,0},{2,3},{3,2},{4,5},{5,4},{6,7},{7,6},{8,9},{9,8},{10,11... | collective-permute-start | bytes 110600 | tf_op jit(solution)/shard_map/ppermute | solution.py:167
  40.4 9.4 %collective-permute-start.13 = (f32[288,128]{1,0:T(8,128)S(1)}, f32[288,128]{1,0:T(8,128)S(1)}, u32[]{:S(2)}, u32[]{:S(2)}) collective-permute-start(f32[288,128]{1,0:T(8,128)S(1)} %pad_maximum_fusion.1), channel_id=1, source_target_pairs={{0,4},{4,0},{8,12},{12,8},{16,20},{20,16},{24,28},{28,24},{32,36},... | collective-permute-start | bytes 442376 | tf_op jit(solution)/shard_map/ppermute | solution.py:168

commit v4 on v3

--- a/solution.py
+++ b/solution.py
@@ -162,24 +162,32 @@
 
 
 def flip(x, axis, mask):
-    step = {"z": 8, "y": 2, "core": 1}
-    if axis == "x":
-        return lax.ppermute(x, "batch", [(i, i ^ mask) for i in range(lax.axis_size("batch"))])
-    return lax.ppermute(x, "rows", [(i, i ^ (mask * step[axis])) for i in range(lax.axis_size("rows"))])
+    step = {"z": 8, "y": 2}
+    width = lax.axis_size("batch")
+    pairs = []
+    for row in range(lax.axis_size("rows")):
+        for col in range(width):
+            to_row, to_col = (row, col ^ mask) if axis == "x" else (row ^ (mask * step[axis]), col)
+            pairs.append((row * width + col, (to_row ^ (mask & 1)) * width + to_col))
+    return lax.ppermute(x, ("rows", "batch"), pairs)
+
+
+def other_core(x):
+    return lax.ppermute(x, "rows", [(i, i ^ 1) for i in range(lax.axis_size("rows"))])
 
 
 def total(x):
-    core = lax.axis_index("rows") % 2
-    here = lax.axis_index("batch")
+    row, here = lax.axis_index("rows"), lax.axis_index("batch")
+    role = (row ^ (row // 2) ^ (row // 8) ^ here) % 2
     half = x.shape[0] // 2
-    x = lax.dynamic_slice_in_dim(x, core * half, half, 0) + flip(
-        lax.dynamic_slice_in_dim(x, (1 - core) * half, half, 0), "core", 1
+    x = lax.dynamic_slice_in_dim(x, role * half, half, 0) + other_core(
+        lax.dynamic_slice_in_dim(x, (1 - role) * half, half, 0)
     )
     part = half // 4
     got = [flip(lax.dynamic_slice_in_dim(x, (here ^ d) * part, part, 0), "x", d) for d in (1, 2, 3)]
     x = (lax.dynamic_slice_in_dim(x, here * part, part, 0) + got[1]) + (got[0] + got[2])
-    x = x + flip(x, "y", 1)
-    x = x + flip(x, "y", 3)
+    got = [flip(x, "y", d) for d in (1, 2, 3)]
+    x = (x + got[1]) + (got[0] + got[2])
     x = x + flip(x, "z", 7)
     got = [flip(x, "z", d) for d in (1, 2, 3)]
     x = (x + got[1]) + (got[0] + got[2])
@@ -191,8 +199,8 @@
         ],
         axis=0,
     )
-    y = flip(x, "core", 1)
-    return jnp.concatenate([jnp.where(core == 0, x, y), jnp.where(core == 0, y, x)], axis=0)
+    y = other_core(x)
+    return jnp.concatenate([jnp.where(role == 0, x, y), jnp.where(role == 0, y, x)], axis=0)
 
 
 def shards(velocity):

time: 63.3 us -> 60.1 us (0.949)
  starting transfers between devices: 29.8 us -> 26.2 us
    ppermute x14 -> x15, starting transfers between devices: 29.8 us -> 26.2 us  [the longest x13 22.1 us: flip(): return lax.ppermute(x, ('rows', 'batch'), pairs)]
    ppermute x14 -> x15, waiting for transfers between devices: 15.1 us -> 15.5 us  [the longest x13 13.5 us: flip(): return lax.ppermute(x, ('rows', 'batch'), pairs)]
  transfers between devices with their start and end apart: 14 -> 15, of which waited for: 12 -> 13; matrix products, arithmetic and copies ran while one was open for 0% -> 0% of each run, Pallas kernels for 0% -> 0%
where the time goes in v4:
time: 60.1 us; the launch traced here: 60 us
  starting transfers between devices  26.2 us (44%)
  Pallas kernels  17.2 us (29%)
  waiting for transfers between devices  15.5 us (26%)
  between operations  0.92 us (2%)
    ppermute x13, starting transfers between devices, flip(): return lax.ppermute(x, ('rows', 'batch'), pairs)  22.1 us
    ppermute x13, waiting for transfers between devices, flip(): return lax.ppermute(x, ('rows', 'batch'), pairs)  13.5 us
    pallas_call x1, Pallas kernels, shards(): pl.pallas_call(lambda *refs: modes_kernel(1.0 / stack, planes, width, *re...  13.3 us
    ppermute x2, starting transfers between devices, other_core(): lax.ppermute(x, 'rows', [(i, i ^ 1) for i in range(lax.axis_size('rows'))])  4.13 us
    pallas_call x1, Pallas kernels, shards(): pl.pallas_call(lambda *refs: gram_kernel(planes, width, *refs), in_specs=...  3.97 us
    ppermute x2, waiting for transfers between devices, other_core(): lax.ppermute(x, 'rows', [(i, i ^ 1) for i in range(lax.axis_size('rows'))])  2.01 us
  transfers between devices with their start and end apart: 15, of which 13 were waited for; matrix products, arithmetic and copies ran while one was open for 0% of the time, Pallas kernels for 0%

profile of v4, /device:TPU:1, one launch (start us, length us, event | category | flops | bytes accessed | tf_op | source)
XLA Modules:
  0.0 60.0 jit_solution(4369734890673874942)
XLA Ops:
  0.7 4.0 %gram.1 = f32[576,128]{1,0:T(8,128)S(1)} custom-call(bf16[8,2048,128]{2,1,0:T(8,128)(2,1)} %refs_1_.1), custom_call_target="tpu_custom_call" | custom-call | tf_op jit(solution)/shard_map/gram/pallas_call | solution.py:212
  4.7 3.3 %collective-permute-start = (f32[288,128]{1,0:T(8,128)S(1)}, f32[288,128]{1,0:T(8,128)S(1)}, u32[]{:S(2)}, u32[]{:S(2)}) collective-permute-start(f32[288,128]{1,0:T(8,128)S(1)} %constant_dynamic-slice_fusion.3), channel_id=1, source_target_pairs={{0,4},{4,0},{8,12},{12,8},{16,20},{20,16},{24,28},{28,24},{32,36},... | collective-permute-start | bytes 442376 | tf_op jit(solution)/shard_map/ppermute | solution.py:176
  8.0 1.0 %collective-permute-done = f32[288,128]{1,0:T(8,128)S(1)} collective-permute-done((f32[288,128]{1,0:T(8,128)S(1)}, f32[288,128]{1,0:T(8,128)S(1)}, u32[]{:S(2)}, u32[]{:S(2)}) %collective-permute-start) | collective-permute-done | bytes 147488 | tf_op jit(solution)/shard_map/ppermute | solution.py:176
  9.1 1.1 %collective-permute-start.1 = (f32[72,128]{1,0:T(8,128)S(1)}, f32[72,128]{1,0:T(8,128)S(1)}, u32[]{:S(2)}, u32[]{:S(2)}) collective-permute-start(f32[72,128]{1,0:T(8,128)S(1)} %get-tuple-element.12), channel_id=1, source_target_pairs={{0,2},{1,3},{2,0},{3,1},{4,6},{5,7},{6,4},{7,5},{8,10},{9,11},{10,... | collective-permute-start | bytes 110600 | tf_op jit(solution)/shard_map/ppermute | solution.py:172
  10.2 1.4 %collective-permute-start.3 = (f32[72,128]{1,0:T(8,128)S(1)}, f32[72,128]{1,0:T(8,128)S(1)}, u32[]{:S(2)}, u32[]{:S(2)}) collective-permute-start(f32[72,128]{1,0:T(8,128)S(1)} %get-tuple-element.13), channel_id=1, source_target_pairs={{0,7},{1,6},{2,5},{3,4},{4,3},{5,2},{6,1},{7,0},{8,15},{9,14},{10,... | collective-permute-start | bytes 110600 | tf_op jit(solution)/shard_map/ppermute | solution.py:172
  11.6 0.5 collective-permute-start.2
  12.1 1.4 %collective-permute-done.1 = f32[72,128]{1,0:T(8,128)S(1)} collective-permute-done((f32[72,128]{1,0:T(8,128)S(1)}, f32[72,128]{1,0:T(8,128)S(1)}, u32[]{:S(2)}, u32[]{:S(2)}) %collective-permute-start.1) | collective-permute-done | bytes 36896 | tf_op jit(solution)/shard_map/ppermute | solution.py:172
  13.5 1.9 %collective-permute-done.3 = f32[72,128]{1,0:T(8,128)S(1)} collective-permute-done((f32[72,128]{1,0:T(8,128)S(1)}, f32[72,128]{1,0:T(8,128)S(1)}, u32[]{:S(2)}, u32[]{:S(2)}) %collective-permute-start.3) | collective-permute-done | bytes 36896 | tf_op jit(solution)/shard_map/ppermute | solution.py:172
  15.4 0.0 collective-permute-done.2
  15.4 3.1 %collective-permute-start.6 = (f32[72,128]{1,0:T(8,128)S(1)}, f32[72,128]{1,0:T(8,128)S(1)}, u32[]{:S(2)}, u32[]{:S(2)}) collective-permute-start(f32[72,128]{1,0:T(8,128)S(1)} %add_add_fusion.2), channel_id=1, source_target_pairs={{0,28},{1,29},{2,30},{3,31},{4,24},{5,25},{6,26},{7,27},{8,20},{9,... | collective-permute-start | bytes 110600 | tf_op jit(solution)/shard_map/ppermute | solution.py:172
  18.5 0.0 collective-permute-start.5
  18.5 1.3 %collective-permute-start.4 = (f32[72,128]{1,0:T(8,128)S(1)}, f32[72,128]{1,0:T(8,128)S(1)}, u32[]{:S(2)}, u32[]{:S(2)}) collective-permute-start(f32[72,128]{1,0:T(8,128)S(1)} %add_add_fusion.2), channel_id=1, source_target_pairs={{0,16},{1,17},{2,18},{3,19},{4,20},{5,21},{6,22},{7,23},{8,24},{9,... | collective-permute-start | bytes 110600 | tf_op jit(solution)/shard_map/ppermute | solution.py:172
  19.8 0.4 collective-permute-done.6
  20.2 1.9 %collective-permute-done.5 = f32[72,128]{1,0:T(8,128)S(1)} collective-permute-done((f32[72,128]{1,0:T(8,128)S(1)}, f32[72,128]{1,0:T(8,128)S(1)}, u32[]{:S(2)}, u32[]{:S(2)}) %collective-permute-start.5) | collective-permute-done | bytes 36896 | tf_op jit(solution)/shard_map/ppermute | solution.py:172
  22.1 0.7 %collective-permute-done.4 = f32[72,128]{1,0:T(8,128)S(1)} collective-permute-done((f32[72,128]{1,0:T(8,128)S(1)}, f32[72,128]{1,0:T(8,128)S(1)}, u32[]{:S(2)}, u32[]{:S(2)}) %collective-permute-start.4) | collective-permute-done | bytes 36896 | tf_op jit(solution)/shard_map/ppermute | solution.py:172
  22.8 7.0 %collective-permute-start.7 = (f32[72,128]{1,0:T(8,128)S(1)}, f32[72,128]{1,0:T(8,128)S(1)}, u32[]{:S(2)}, u32[]{:S(2)}) collective-permute-start(f32[72,128]{1,0:T(8,128)S(1)} %add_add_fusion.1), channel_id=1, source_target_pairs={{0,228},{1,229},{2,230},{3,231},{4,224},{5,225},{6,226},{7,227},{8... | collective-permute-start | bytes 110600 | tf_op jit(solution)/shard_map/ppermute | solution.py:172
  29.8 1.6 %collective-permute-done.7 = f32[72,128]{1,0:T(8,128)S(1)} collective-permute-done((f32[72,128]{1,0:T(8,128)S(1)}, f32[72,128]{1,0:T(8,128)S(1)}, u32[]{:S(2)}, u32[]{:S(2)}) %collective-permute-start.7) | collective-permute-done | bytes 36896 | tf_op jit(solution)/shard_map/ppermute | solution.py:172
  31.4 1.7 %collective-permute-start.10 = (f32[72,128]{1,0:T(8,128)S(1)}, f32[72,128]{1,0:T(8,128)S(1)}, u32[]{:S(2)}, u32[]{:S(2)}) collective-permute-start(f32[72,128]{1,0:T(8,128)S(1)} %add.71), channel_id=1, source_target_pairs={{0,100},{1,101},{2,102},{3,103},{4,96},{5,97},{6,98},{7,99},{8,108... | collective-permute-start | bytes 110600 | tf_op jit(solution)/shard_map/ppermute | solution.py:172
  33.2 1.0 %collective-permute-start.9 = (f32[72,128]{1,0:T(8,128)S(1)}, f32[72,128]{1,0:T(8,128)S(1)}, u32[]{:S(2)}, u32[]{:S(2)}) collective-permute-start(f32[72,128]{1,0:T(8,128)S(1)} %add.71), channel_id=1, source_target_pairs={{0,36},{1,37},{2,38},{3,39},{4,32},{5,33},{6,34},{7,35},{8,44},{9,... | collective-permute-start | bytes 110600 | tf_op jit(solution)/shard_map/ppermute | solution.py:172
  34.1 1.1 %collective-permute-start.8 = (f32[72,128]{1,0:T(8,128)S(1)}, f32[72,128]{1,0:T(8,128)S(1)}, u32[]{:S(2)}, u32[]{:S(2)}) collective-permute-start(f32[72,128]{1,0:T(8,128)S(1)} %add.71), channel_id=1, source_target_pairs={{0,64},{1,65},{2,66},{3,67},{4,68},{5,69},{6,70},{7,71},{8,72},{9,... | collective-permute-start | bytes 110600 | tf_op jit(solution)/shard_map/ppermute | solution.py:172
  35.3 1.5 %collective-permute-done.10 = f32[72,128]{1,0:T(8,128)S(1)} collective-permute-done((f32[72,128]{1,0:T(8,128)S(1)}, f32[72,128]{1,0:T(8,128)S(1)}, u32[]{:S(2)}, u32[]{:S(2)}) %collective-permute-start.10) | collective-permute-done | bytes 36896 | tf_op jit(solution)/shard_map/ppermute | solution.py:172
  36.7 0.7 %collective-permute-done.9 = f32[72,128]{1,0:T(8,128)S(1)} collective-permute-done((f32[72,128]{1,0:T(8,128)S(1)}, f32[72,128]{1,0:T(8,128)S(1)}, u32[]{:S(2)}, u32[]{:S(2)}) %collective-permute-start.9) | collective-permute-done | bytes 36896 | tf_op jit(solution)/shard_map/ppermute | solution.py:172
  37.5 0.4 collective-permute-done.8
  37.8 2.5 %collective-permute-start.13 = (f32[72,128]{1,0:T(8,128)S(1)}, f32[72,128]{1,0:T(8,128)S(1)}, u32[]{:S(2)}, u32[]{:S(2)}) collective-permute-start(f32[72,128]{1,0:T(8,128)S(1)} %add_add_fusion), channel_id=1, source_target_pairs={{0,7},{1,6},{2,5},{3,4},{4,3},{5,2},{6,1},{7,0},{8,15},{9,14},{10,... | collective-permute-start | bytes 110600 | tf_op jit(solution)/shard_map/ppermute | solution.py:172
  40.4 0.2 collective-permute-start.12
  40.6 1.1 %collective-permute-start.11 = (f32[72,128]{1,0:T(8,128)S(1)}, f32[72,128]{1,0:T(8,128)S(1)}, u32[]{:S(2)}, u32[]{:S(2)}) collective-permute-start(f32[72,128]{1,0:T(8,128)S(1)} %add_add_fusion), channel_id=1, source_target_pairs={{0,5},{1,4},{2,7},{3,6},{4,1},{5,0},{6,3},{7,2},{8,13},{9,12},{10,... | collective-permute-start | bytes 110600 | tf_op jit(solution)/shard_map/ppermute | solution.py:172
  41.7 0.8 %collective-permute-done.13 = f32[72,128]{1,0:T(8,128)S(1)} collective-permute-done((f32[72,128]{1,0:T(8,128)S(1)}, f32[72,128]{1,0:T(8,128)S(1)}, u32[]{:S(2)}, u32[]{:S(2)}) %collective-permute-start.13) | collective-permute-done | bytes 36896 | tf_op jit(solution)/shard_map/ppermute | solution.py:172
  42.5 2.2 %collective-permute-done.12 = f32[72,128]{1,0:T(8,128)S(1)} collective-permute-done((f32[72,128]{1,0:T(8,128)S(1)}, f32[72,128]{1,0:T(8,128)S(1)}, u32[]{:S(2)}, u32[]{:S(2)}) %collective-permute-start.12) | collective-permute-done | bytes 36896 | tf_op jit(solution)/shard_map/ppermute | solution.py:172
  44.7 0.0 collective-permute-done.11
  44.8 0.8 %collective-permute-start.14 = (f32[288,128]{1,0:T(8,128)S(1)}, f32[288,128]{1,0:T(8,128)S(1)}, u32[]{:S(2)}, u32[]{:S(2)}) collective-permute-start(f32[288,128]{1,0:T(8,128)S(1)} %pad_maximum_fusion.1), channel_id=1, source_target_pairs={{0,4},{4,0},{8,12},{12,8},{16,20},{20,16},{24,28},{28,24},{32,36},... | collective-permute-start | bytes 442376 | tf_op jit(solution)/shard_map/ppermute | solution.py:176
  45.6 1.0 %collective-permute-done.14 = f32[288,128]{1,0:T(8,128)S(1)} collective-permute-done((f32[288,128]{1,0:T(8,128)S(1)}, f32[288,128]{1,0:T(8,128)S(1)}, u32[]{:S(2)}, u32[]{:S(2)}) %collective-permute-start.14) | collective-permute-done | bytes 147488 | tf_op jit(solution)/shard_map/ppermute | solution.py:176
  46.6 13.3 %factor_modes.1 = (f32[1024,128]{1,0:T(8,128)}, f32[8,2048,128]{2,1,0:T(8,128)}) custom-call(f32[576,128]{1,0:T(8,128)S(1)} %pad_maximum_fusion.refs_0_, bf16[8,2048,128]{2,1,0:T(8,128)(2,1)} %refs_1_.1), custom_call_target="tpu_custom_call" | custom-call | tf_op jit(solution)/shard_map/factor_modes/pallas_call | solution.py:226
  (11 shorter events, 0.2 us)
Async XLA Ops:
  4.7 4.3 %collective-permute-start = (f32[288,128]{1,0:T(8,128)S(1)}, f32[288,128]{1,0:T(8,128)S(1)}, u32[]{:S(2)}, u32[]{:S(2)}) collective-permute-start(f32[288,128]{1,0:T(8,128)S(1)} %constant_dynamic-slice_fusion.3), channel_id=1, source_target_pairs={{0,4},{4,0},{8,12},{12,8},{16,20},{20,16},{24,28},{28,24},{32,36},... | collective-permute-start | bytes 442376 | tf_op jit(solution)/shard_map/ppermute | solution.py:176
  9.1 4.4 %collective-permute-start.1 = (f32[72,128]{1,0:T(8,128)S(1)}, f32[72,128]{1,0:T(8,128)S(1)}, u32[]{:S(2)}, u32[]{:S(2)}) collective-permute-start(f32[72,128]{1,0:T(8,128)S(1)} %get-tuple-element.12), channel_id=1, source_target_pairs={{0,2},{1,3},{2,0},{3,1},{4,6},{5,7},{6,4},{7,5},{8,10},{9,11},{10,... | collective-permute-start | bytes 110600 | tf_op jit(solution)/shard_map/ppermute | solution.py:172
  10.2 5.2 %collective-permute-start.3 = (f32[72,128]{1,0:T(8,128)S(1)}, f32[72,128]{1,0:T(8,128)S(1)}, u32[]{:S(2)}, u32[]{:S(2)}) collective-permute-start(f32[72,128]{1,0:T(8,128)S(1)} %get-tuple-element.13), channel_id=1, source_target_pairs={{0,7},{1,6},{2,5},{3,4},{4,3},{5,2},{6,1},{7,0},{8,15},{9,14},{10,... | collective-permute-start | bytes 110600 | tf_op jit(solution)/shard_map/ppermute | solution.py:172
  11.6 3.8 %collective-permute-start.2 = (f32[72,128]{1,0:T(8,128)S(1)}, f32[72,128]{1,0:T(8,128)S(1)}, u32[]{:S(2)}, u32[]{:S(2)}) collective-permute-start(f32[72,128]{1,0:T(8,128)S(1)} %get-tuple-element.14), channel_id=1, source_target_pairs={{0,5},{1,4},{2,7},{3,6},{4,1},{5,0},{6,3},{7,2},{8,13},{9,12},{10,... | collective-permute-start | bytes 110600 | tf_op jit(solution)/shard_map/ppermute | solution.py:172
  15.4 4.8 %collective-permute-start.6 = (f32[72,128]{1,0:T(8,128)S(1)}, f32[72,128]{1,0:T(8,128)S(1)}, u32[]{:S(2)}, u32[]{:S(2)}) collective-permute-start(f32[72,128]{1,0:T(8,128)S(1)} %add_add_fusion.2), channel_id=1, source_target_pairs={{0,28},{1,29},{2,30},{3,31},{4,24},{5,25},{6,26},{7,27},{8,20},{9,... | collective-permute-start | bytes 110600 | tf_op jit(solution)/shard_map/ppermute | solution.py:172
  18.5 3.6 %collective-permute-start.5 = (f32[72,128]{1,0:T(8,128)S(1)}, f32[72,128]{1,0:T(8,128)S(1)}, u32[]{:S(2)}, u32[]{:S(2)}) collective-permute-start(f32[72,128]{1,0:T(8,128)S(1)} %add_add_fusion.2), channel_id=1, source_target_pairs={{0,12},{1,13},{2,14},{3,15},{4,8},{5,9},{6,10},{7,11},{8,4},{9,5},... | collective-permute-start | bytes 110600 | tf_op jit(solution)/shard_map/ppermute | solution.py:172
  18.5 4.3 %collective-permute-start.4 = (f32[72,128]{1,0:T(8,128)S(1)}, f32[72,128]{1,0:T(8,128)S(1)}, u32[]{:S(2)}, u32[]{:S(2)}) collective-permute-start(f32[72,128]{1,0:T(8,128)S(1)} %add_add_fusion.2), channel_id=1, source_target_pairs={{0,16},{1,17},{2,18},{3,19},{4,20},{5,21},{6,22},{7,23},{8,24},{9,... | collective-permute-start | bytes 110600 | tf_op jit(solution)/shard_map/ppermute | solution.py:172
  22.8 8.6 %collective-permute-start.7 = (f32[72,128]{1,0:T(8,128)S(1)}, f32[72,128]{1,0:T(8,128)S(1)}, u32[]{:S(2)}, u32[]{:S(2)}) collective-permute-start(f32[72,128]{1,0:T(8,128)S(1)} %add_add_fusion.1), channel_id=1, source_target_pairs={{0,228},{1,229},{2,230},{3,231},{4,224},{5,225},{6,226},{7,227},{8... | collective-permute-start | bytes 110600 | tf_op jit(solution)/shard_map/ppermute | solution.py:172
  31.4 5.3 %collective-permute-start.10 = (f32[72,128]{1,0:T(8,128)S(1)}, f32[72,128]{1,0:T(8,128)S(1)}, u32[]{:S(2)}, u32[]{:S(2)}) collective-permute-start(f32[72,128]{1,0:T(8,128)S(1)} %add.71), channel_id=1, source_target_pairs={{0,100},{1,101},{2,102},{3,103},{4,96},{5,97},{6,98},{7,99},{8,108... | collective-permute-start | bytes 110600 | tf_op jit(solution)/shard_map/ppermute | solution.py:172
  33.2 4.3 %collective-permute-start.9 = (f32[72,128]{1,0:T(8,128)S(1)}, f32[72,128]{1,0:T(8,128)S(1)}, u32[]{:S(2)}, u32[]{:S(2)}) collective-permute-start(f32[72,128]{1,0:T(8,128)S(1)} %add.71), channel_id=1, source_target_pairs={{0,36},{1,37},{2,38},{3,39},{4,32},{5,33},{6,34},{7,35},{8,44},{9,... | collective-permute-start | bytes 110600 | tf_op jit(solution)/shard_map/ppermute | solution.py:172
  34.1 3.7 %collective-permute-start.8 = (f32[72,128]{1,0:T(8,128)S(1)}, f32[72,128]{1,0:T(8,128)S(1)}, u32[]{:S(2)}, u32[]{:S(2)}) collective-permute-start(f32[72,128]{1,0:T(8,128)S(1)} %add.71), channel_id=1, source_target_pairs={{0,64},{1,65},{2,66},{3,67},{4,68},{5,69},{6,70},{7,71},{8,72},{9,... | collective-permute-start | bytes 110600 | tf_op jit(solution)/shard_map/ppermute | solution.py:172
  37.8 4.7 %collective-permute-start.13 = (f32[72,128]{1,0:T(8,128)S(1)}, f32[72,128]{1,0:T(8,128)S(1)}, u32[]{:S(2)}, u32[]{:S(2)}) collective-permute-start(f32[72,128]{1,0:T(8,128)S(1)} %add_add_fusion), channel_id=1, source_target_pairs={{0,7},{1,6},{2,5},{3,4},{4,3},{5,2},{6,1},{7,0},{8,15},{9,14},{10,... | collective-permute-start | bytes 110600 | tf_op jit(solution)/shard_map/ppermute | solution.py:172
  40.4 4.3 %collective-permute-start.12 = (f32[72,128]{1,0:T(8,128)S(1)}, f32[72,128]{1,0:T(8,128)S(1)}, u32[]{:S(2)}, u32[]{:S(2)}) collective-permute-start(f32[72,128]{1,0:T(8,128)S(1)} %add_add_fusion), channel_id=1, source_target_pairs={{0,2},{1,3},{2,0},{3,1},{4,6},{5,7},{6,4},{7,5},{8,10},{9,11},{10,... | collective-permute-start | bytes 110600 | tf_op jit(solution)/shard_map/ppermute | solution.py:172
  40.6 4.1 %collective-permute-start.11 = (f32[72,128]{1,0:T(8,128)S(1)}, f32[72,128]{1,0:T(8,128)S(1)}, u32[]{:S(2)}, u32[]{:S(2)}) collective-permute-start(f32[72,128]{1,0:T(8,128)S(1)} %add_add_fusion), channel_id=1, source_target_pairs={{0,5},{1,4},{2,7},{3,6},{4,1},{5,0},{6,3},{7,2},{8,13},{9,12},{10,... | collective-permute-start | bytes 110600 | tf_op jit(solution)/shard_map/ppermute | solution.py:172
  44.8 1.8 %collective-permute-start.14 = (f32[288,128]{1,0:T(8,128)S(1)}, f32[288,128]{1,0:T(8,128)S(1)}, u32[]{:S(2)}, u32[]{:S(2)}) collective-permute-start(f32[288,128]{1,0:T(8,128)S(1)} %pad_maximum_fusion.1), channel_id=1, source_target_pairs={{0,4},{4,0},{8,12},{12,8},{16,20},{20,16},{24,28},{28,24},{32,36},... | collective-permute-start | bytes 442376 | tf_op jit(solution)/shard_map/ppermute | solution.py:176

commit v5 on v4

--- a/solution.py
+++ b/solution.py
@@ -6,8 +6,9 @@
 from jax.sharding import PartitionSpec as P
 
 BLOCK = 8
-PANEL = 16
+PANEL = 2 * BLOCK
 GROUP = 16
+TILE = 256
 LIMIT = 51 * 1024 * 1024
 
 
@@ -77,34 +78,35 @@
 
     for first in range(0, width, PANEL):
         last = first + PANEL
-        for start in range(first, last, BLOCK):
+        for start in (first, first + BLOCK):
             kept = (lanes < first) | (lanes >= start)
-            inside = (lanes >= start) & (lanes < start + BLOCK)
             rows = [jnp.where(kept, row(x_ref, start + i), 0.0) for i in range(BLOCK)]
-            for k in range(first, start):
-                source = row(p_ref, k)
-                for i in range(BLOCK):
-                    rows[i] = rows[i] - lane(source, start + i) * source
-                p_ref[k * planes : (k + 1) * planes, :] = jnp.where(inside, 0.0, source)
-            cell = {(i, j): lane(rows[i], start + j) for i in range(BLOCK) for j in range(i, BLOCK)}
+            if start > first:
+                inside = (lanes >= start) & (lanes < start + BLOCK)
+                for k in range(BLOCK):
+                    for i in range(BLOCK):
+                        rows[i] = rows[i] - cell[k, BLOCK + i] * older[k]
+                    p_ref[(first + k) * planes : (first + k + 1) * planes, :] = jnp.where(inside, 0.0, older[k])
+            columns = last - start
+            cell = {(i, j): lane(rows[i], start + j) for i in range(BLOCK) for j in range(i, columns)}
+            older = []
             for k in range(BLOCK):
-                pivot = cell[k, k]
-                root = lax.rsqrt(pivot)
-                root = root * (1.5 - 0.5 * pivot * root * root)
-                for j in range(k + 1, BLOCK):
+                root = lax.rsqrt(cell[k, k])
+                for j in range(k + 1, columns):
                     cell[k, j] = cell[k, j] * root
                 for i in range(k + 1, BLOCK):
-                    for j in range(i, BLOCK):
+                    for j in range(i, columns):
                         cell[i, j] = cell[i, j] - cell[k, i] * cell[k, j]
                 here = lanes == start + k
                 whole = rows[k] * root
                 u_ref[pl.ds(start + k, planes, stride=width), :] = jnp.where(lanes >= start + k, whole, 0.0)
                 whole = jnp.where(here, root, whole)
-                p_ref[(start + k) * planes : (start + k + 1) * planes, :] = jnp.where(
-                    (lanes <= start + k) | (lanes >= start + BLOCK), whole, 0.0
-                )
+                older.append(jnp.where((lanes <= start + k) | (lanes >= start + BLOCK), whole, 0.0))
                 for i in range(k + 1, BLOCK):
                     rows[i] = jnp.where(here, 0.0, rows[i]) - cell[k, i] * whole
+            if start > first:
+                for k in range(BLOCK):
+                    p_ref[(start + k) * planes : (start + k + 1) * planes, :] = older[k]
         if last == width:
             break
         done = (wide[last:, :] >= first) & (wide[last:, :] < last)
@@ -126,8 +128,11 @@
     def fetch(p):
         return pltpu.make_async_copy(v_hbm.at[p], v_ref.at[p], in_sem.at[p])
 
-    def put(p):
-        return pltpu.make_async_copy(m_ref.at[p], m_hbm.at[p], out_sem.at[p])
+    tiles = v_ref.shape[1] // TILE
+
+    def put(p, t):
+        at = pl.ds(t * TILE, TILE)
+        return pltpu.make_async_copy(m_ref.at[p, at], m_hbm.at[p, at], out_sem.at[p * tiles + t])
 
     for p in range(planes):
         fetch(p).start()
@@ -147,18 +152,20 @@
             axis=0,
         )
         fetch(p).wait()
-        v = v_ref[p]
-        both = lax.dot_general(
-            jnp.concatenate([v, v], axis=1),
-            weights,
-            (((1,), (1,)), ((), ())),
-            preferred_element_type=jnp.float32,
-        )
-        m_ref[p] = both[:, :width] + both[:, width:]
-        put(p).start()
+        for t in range(tiles):
+            v = v_ref[p, t * TILE : (t + 1) * TILE, :]
+            both = lax.dot_general(
+                jnp.concatenate([v, v], axis=1),
+                weights,
+                (((1,), (1,)), ((), ())),
+                preferred_element_type=jnp.float32,
+            )
+            m_ref[p, t * TILE : (t + 1) * TILE, :] = both[:, :width] + both[:, width:]
+            put(p, t).start()
     put_factor.wait()
     for p in range(planes):
-        put(p).wait()
+        for t in range(tiles):
+            put(p, t).wait()
 
 
 def flip(x, axis, mask):
@@ -238,7 +245,7 @@
             pltpu.VMEM((planes, rows_dev, width), jnp.bfloat16),
             pltpu.VMEM((planes, rows_dev, width), jnp.float32),
             pltpu.SemaphoreType.DMA((planes,)),
-            pltpu.SemaphoreType.DMA((planes,)),
+            pltpu.SemaphoreType.DMA((planes * (rows_dev // TILE),)),
             pltpu.SemaphoreType.DMA,
         ],
         compiler_params=pltpu.CompilerParams(vmem_limit_bytes=LIMIT),

time: 60.1 us -> 56.9 us (0.947)
  Pallas kernels: 17.2 us -> 14 us
    pallas_call x1, Pallas kernels: 13.3 us -> 10 us  [shards(): pl.pallas_call(lambda *refs: modes_kernel(1.0 / stack, planes, width, *re...]
where the time goes in v5:
time: 56.9 us; the launch traced here: 56.8 us
  starting transfers between devices  26.2 us (46%)
  waiting for transfers between devices  15.5 us (27%)
  Pallas kernels  14 us (25%)
  between operations  0.92 us (2%)
    ppermute x13, starting transfers between devices, flip(): return lax.ppermute(x, ('rows', 'batch'), pairs)  22.1 us
    ppermute x13, waiting for transfers between devices, flip(): return lax.ppermute(x, ('rows', 'batch'), pairs)  13.5 us
    pallas_call x1, Pallas kernels, shards(): pl.pallas_call(lambda *refs: modes_kernel(1.0 / stack, planes, width, *re...  10 us
    ppermute x2, starting transfers between devices, other_core(): lax.ppermute(x, 'rows', [(i, i ^ 1) for i in range(lax.axis_size('rows'))])  4.13 us
    pallas_call x1, Pallas kernels, shards(): pl.pallas_call(lambda *refs: gram_kernel(planes, width, *refs), in_specs=...  3.97 us
    ppermute x2, waiting for transfers between devices, other_core(): lax.ppermute(x, 'rows', [(i, i ^ 1) for i in range(lax.axis_size('rows'))])  2.01 us
  transfers between devices with their start and end apart: 15, of which 13 were waited for; matrix products, arithmetic and copies ran while one was open for 0% of the time, Pallas kernels for 0%

profile of v5, /device:TPU:1, one launch (start us, length us, event | category | flops | bytes accessed | tf_op | source)
XLA Modules:
  0.0 56.8 jit_solution(630919678556680518)
XLA Ops:
  0.7 4.0 %gram.1 = f32[576,128]{1,0:T(8,128)S(1)} custom-call(bf16[8,2048,128]{2,1,0:T(8,128)(2,1)} %refs_1_.1), custom_call_target="tpu_custom_call" | custom-call | tf_op jit(solution)/shard_map/gram/pallas_call | solution.py:219
  4.7 3.3 %collective-permute-start = (f32[288,128]{1,0:T(8,128)S(1)}, f32[288,128]{1,0:T(8,128)S(1)}, u32[]{:S(2)}, u32[]{:S(2)}) collective-permute-start(f32[288,128]{1,0:T(8,128)S(1)} %constant_dynamic-slice_fusion.3), channel_id=1, source_target_pairs={{0,4},{4,0},{8,12},{12,8},{16,20},{20,16},{24,28},{28,24},{32,36},... | collective-permute-start | bytes 442376 | tf_op jit(solution)/shard_map/ppermute | solution.py:183
  8.0 1.0 %collective-permute-done = f32[288,128]{1,0:T(8,128)S(1)} collective-permute-done((f32[288,128]{1,0:T(8,128)S(1)}, f32[288,128]{1,0:T(8,128)S(1)}, u32[]{:S(2)}, u32[]{:S(2)}) %collective-permute-start) | collective-permute-done | bytes 147488 | tf_op jit(solution)/shard_map/ppermute | solution.py:183
  9.1 1.1 %collective-permute-start.1 = (f32[72,128]{1,0:T(8,128)S(1)}, f32[72,128]{1,0:T(8,128)S(1)}, u32[]{:S(2)}, u32[]{:S(2)}) collective-permute-start(f32[72,128]{1,0:T(8,128)S(1)} %get-tuple-element.12), channel_id=1, source_target_pairs={{0,2},{1,3},{2,0},{3,1},{4,6},{5,7},{6,4},{7,5},{8,10},{9,11},{10,... | collective-permute-start | bytes 110600 | tf_op jit(solution)/shard_map/ppermute | solution.py:179
  10.2 1.4 %collective-permute-start.3 = (f32[72,128]{1,0:T(8,128)S(1)}, f32[72,128]{1,0:T(8,128)S(1)}, u32[]{:S(2)}, u32[]{:S(2)}) collective-permute-start(f32[72,128]{1,0:T(8,128)S(1)} %get-tuple-element.13), channel_id=1, source_target_pairs={{0,7},{1,6},{2,5},{3,4},{4,3},{5,2},{6,1},{7,0},{8,15},{9,14},{10,... | collective-permute-start | bytes 110600 | tf_op jit(solution)/shard_map/ppermute | solution.py:179
  11.6 0.5 collective-permute-start.2
  12.1 1.4 %collective-permute-done.1 = f32[72,128]{1,0:T(8,128)S(1)} collective-permute-done((f32[72,128]{1,0:T(8,128)S(1)}, f32[72,128]{1,0:T(8,128)S(1)}, u32[]{:S(2)}, u32[]{:S(2)}) %collective-permute-start.1) | collective-permute-done | bytes 36896 | tf_op jit(solution)/shard_map/ppermute | solution.py:179
  13.5 1.9 %collective-permute-done.3 = f32[72,128]{1,0:T(8,128)S(1)} collective-permute-done((f32[72,128]{1,0:T(8,128)S(1)}, f32[72,128]{1,0:T(8,128)S(1)}, u32[]{:S(2)}, u32[]{:S(2)}) %collective-permute-start.3) | collective-permute-done | bytes 36896 | tf_op jit(solution)/shard_map/ppermute | solution.py:179
  15.4 0.0 collective-permute-done.2
  15.4 3.1 %collective-permute-start.6 = (f32[72,128]{1,0:T(8,128)S(1)}, f32[72,128]{1,0:T(8,128)S(1)}, u32[]{:S(2)}, u32[]{:S(2)}) collective-permute-start(f32[72,128]{1,0:T(8,128)S(1)} %add_add_fusion.2), channel_id=1, source_target_pairs={{0,28},{1,29},{2,30},{3,31},{4,24},{5,25},{6,26},{7,27},{8,20},{9,... | collective-permute-start | bytes 110600 | tf_op jit(solution)/shard_map/ppermute | solution.py:179
  18.5 0.0 collective-permute-start.5
  18.5 1.3 %collective-permute-start.4 = (f32[72,128]{1,0:T(8,128)S(1)}, f32[72,128]{1,0:T(8,128)S(1)}, u32[]{:S(2)}, u32[]{:S(2)}) collective-permute-start(f32[72,128]{1,0:T(8,128)S(1)} %add_add_fusion.2), channel_id=1, source_target_pairs={{0,16},{1,17},{2,18},{3,19},{4,20},{5,21},{6,22},{7,23},{8,24},{9,... | collective-permute-start | bytes 110600 | tf_op jit(solution)/shard_map/ppermute | solution.py:179
  19.8 0.4 collective-permute-done.6
  20.2 1.9 %collective-permute-done.5 = f32[72,128]{1,0:T(8,128)S(1)} collective-permute-done((f32[72,128]{1,0:T(8,128)S(1)}, f32[72,128]{1,0:T(8,128)S(1)}, u32[]{:S(2)}, u32[]{:S(2)}) %collective-permute-start.5) | collective-permute-done | bytes 36896 | tf_op jit(solution)/shard_map/ppermute | solution.py:179
  22.1 0.7 %collective-permute-done.4 = f32[72,128]{1,0:T(8,128)S(1)} collective-permute-done((f32[72,128]{1,0:T(8,128)S(1)}, f32[72,128]{1,0:T(8,128)S(1)}, u32[]{:S(2)}, u32[]{:S(2)}) %collective-permute-start.4) | collective-permute-done | bytes 36896 | tf_op jit(solution)/shard_map/ppermute | solution.py:179
  22.8 7.0 %collective-permute-start.7 = (f32[72,128]{1,0:T(8,128)S(1)}, f32[72,128]{1,0:T(8,128)S(1)}, u32[]{:S(2)}, u32[]{:S(2)}) collective-permute-start(f32[72,128]{1,0:T(8,128)S(1)} %add_add_fusion.1), channel_id=1, source_target_pairs={{0,228},{1,229},{2,230},{3,231},{4,224},{5,225},{6,226},{7,227},{8... | collective-permute-start | bytes 110600 | tf_op jit(solution)/shard_map/ppermute | solution.py:179
  29.8 1.6 %collective-permute-done.7 = f32[72,128]{1,0:T(8,128)S(1)} collective-permute-done((f32[72,128]{1,0:T(8,128)S(1)}, f32[72,128]{1,0:T(8,128)S(1)}, u32[]{:S(2)}, u32[]{:S(2)}) %collective-permute-start.7) | collective-permute-done | bytes 36896 | tf_op jit(solution)/shard_map/ppermute | solution.py:179
  31.4 1.7 %collective-permute-start.10 = (f32[72,128]{1,0:T(8,128)S(1)}, f32[72,128]{1,0:T(8,128)S(1)}, u32[]{:S(2)}, u32[]{:S(2)}) collective-permute-start(f32[72,128]{1,0:T(8,128)S(1)} %add.71), channel_id=1, source_target_pairs={{0,100},{1,101},{2,102},{3,103},{4,96},{5,97},{6,98},{7,99},{8,108... | collective-permute-start | bytes 110600 | tf_op jit(solution)/shard_map/ppermute | solution.py:179
  33.2 1.0 %collective-permute-start.9 = (f32[72,128]{1,0:T(8,128)S(1)}, f32[72,128]{1,0:T(8,128)S(1)}, u32[]{:S(2)}, u32[]{:S(2)}) collective-permute-start(f32[72,128]{1,0:T(8,128)S(1)} %add.71), channel_id=1, source_target_pairs={{0,36},{1,37},{2,38},{3,39},{4,32},{5,33},{6,34},{7,35},{8,44},{9,... | collective-permute-start | bytes 110600 | tf_op jit(solution)/shard_map/ppermute | solution.py:179
  34.1 1.1 %collective-permute-start.8 = (f32[72,128]{1,0:T(8,128)S(1)}, f32[72,128]{1,0:T(8,128)S(1)}, u32[]{:S(2)}, u32[]{:S(2)}) collective-permute-start(f32[72,128]{1,0:T(8,128)S(1)} %add.71), channel_id=1, source_target_pairs={{0,64},{1,65},{2,66},{3,67},{4,68},{5,69},{6,70},{7,71},{8,72},{9,... | collective-permute-start | bytes 110600 | tf_op jit(solution)/shard_map/ppermute | solution.py:179
  35.3 1.5 %collective-permute-done.10 = f32[72,128]{1,0:T(8,128)S(1)} collective-permute-done((f32[72,128]{1,0:T(8,128)S(1)}, f32[72,128]{1,0:T(8,128)S(1)}, u32[]{:S(2)}, u32[]{:S(2)}) %collective-permute-start.10) | collective-permute-done | bytes 36896 | tf_op jit(solution)/shard_map/ppermute | solution.py:179
  36.7 0.7 %collective-permute-done.9 = f32[72,128]{1,0:T(8,128)S(1)} collective-permute-done((f32[72,128]{1,0:T(8,128)S(1)}, f32[72,128]{1,0:T(8,128)S(1)}, u32[]{:S(2)}, u32[]{:S(2)}) %collective-permute-start.9) | collective-permute-done | bytes 36896 | tf_op jit(solution)/shard_map/ppermute | solution.py:179
  37.5 0.4 collective-permute-done.8
  37.8 2.5 %collective-permute-start.13 = (f32[72,128]{1,0:T(8,128)S(1)}, f32[72,128]{1,0:T(8,128)S(1)}, u32[]{:S(2)}, u32[]{:S(2)}) collective-permute-start(f32[72,128]{1,0:T(8,128)S(1)} %add_add_fusion), channel_id=1, source_target_pairs={{0,7},{1,6},{2,5},{3,4},{4,3},{5,2},{6,1},{7,0},{8,15},{9,14},{10,... | collective-permute-start | bytes 110600 | tf_op jit(solution)/shard_map/ppermute | solution.py:179
  40.4 0.2 collective-permute-start.12
  40.6 1.1 %collective-permute-start.11 = (f32[72,128]{1,0:T(8,128)S(1)}, f32[72,128]{1,0:T(8,128)S(1)}, u32[]{:S(2)}, u32[]{:S(2)}) collective-permute-start(f32[72,128]{1,0:T(8,128)S(1)} %add_add_fusion), channel_id=1, source_target_pairs={{0,5},{1,4},{2,7},{3,6},{4,1},{5,0},{6,3},{7,2},{8,13},{9,12},{10,... | collective-permute-start | bytes 110600 | tf_op jit(solution)/shard_map/ppermute | solution.py:179
  41.7 0.8 %collective-permute-done.13 = f32[72,128]{1,0:T(8,128)S(1)} collective-permute-done((f32[72,128]{1,0:T(8,128)S(1)}, f32[72,128]{1,0:T(8,128)S(1)}, u32[]{:S(2)}, u32[]{:S(2)}) %collective-permute-start.13) | collective-permute-done | bytes 36896 | tf_op jit(solution)/shard_map/ppermute | solution.py:179
  42.5 2.2 %collective-permute-done.12 = f32[72,128]{1,0:T(8,128)S(1)} collective-permute-done((f32[72,128]{1,0:T(8,128)S(1)}, f32[72,128]{1,0:T(8,128)S(1)}, u32[]{:S(2)}, u32[]{:S(2)}) %collective-permute-start.12) | collective-permute-done | bytes 36896 | tf_op jit(solution)/shard_map/ppermute | solution.py:179
  44.7 0.0 collective-permute-done.11
  44.8 0.8 %collective-permute-start.14 = (f32[288,128]{1,0:T(8,128)S(1)}, f32[288,128]{1,0:T(8,128)S(1)}, u32[]{:S(2)}, u32[]{:S(2)}) collective-permute-start(f32[288,128]{1,0:T(8,128)S(1)} %pad_maximum_fusion.1), channel_id=1, source_target_pairs={{0,4},{4,0},{8,12},{12,8},{16,20},{20,16},{24,28},{28,24},{32,36},... | collective-permute-start | bytes 442376 | tf_op jit(solution)/shard_map/ppermute | solution.py:183
  45.6 1.0 %collective-permute-done.14 = f32[288,128]{1,0:T(8,128)S(1)} collective-permute-done((f32[288,128]{1,0:T(8,128)S(1)}, f32[288,128]{1,0:T(8,128)S(1)}, u32[]{:S(2)}, u32[]{:S(2)}) %collective-permute-start.14) | collective-permute-done | bytes 147488 | tf_op jit(solution)/shard_map/ppermute | solution.py:183
  46.6 10.0 %factor_modes.1 = (f32[1024,128]{1,0:T(8,128)}, f32[8,2048,128]{2,1,0:T(8,128)}) custom-call(f32[576,128]{1,0:T(8,128)S(1)} %pad_maximum_fusion.refs_0_, bf16[8,2048,128]{2,1,0:T(8,128)(2,1)} %refs_1_.1), custom_call_target="tpu_custom_call" | custom-call | tf_op jit(solution)/shard_map/factor_modes/pallas_call | solution.py:233
  (11 shorter events, 0.2 us)
Async XLA Ops:
  4.7 4.3 %collective-permute-start = (f32[288,128]{1,0:T(8,128)S(1)}, f32[288,128]{1,0:T(8,128)S(1)}, u32[]{:S(2)}, u32[]{:S(2)}) collective-permute-start(f32[288,128]{1,0:T(8,128)S(1)} %constant_dynamic-slice_fusion.3), channel_id=1, source_target_pairs={{0,4},{4,0},{8,12},{12,8},{16,20},{20,16},{24,28},{28,24},{32,36},... | collective-permute-start | bytes 442376 | tf_op jit(solution)/shard_map/ppermute | solution.py:183
  9.1 4.4 %collective-permute-start.1 = (f32[72,128]{1,0:T(8,128)S(1)}, f32[72,128]{1,0:T(8,128)S(1)}, u32[]{:S(2)}, u32[]{:S(2)}) collective-permute-start(f32[72,128]{1,0:T(8,128)S(1)} %get-tuple-element.12), channel_id=1, source_target_pairs={{0,2},{1,3},{2,0},{3,1},{4,6},{5,7},{6,4},{7,5},{8,10},{9,11},{10,... | collective-permute-start | bytes 110600 | tf_op jit(solution)/shard_map/ppermute | solution.py:179
  10.2 5.2 %collective-permute-start.3 = (f32[72,128]{1,0:T(8,128)S(1)}, f32[72,128]{1,0:T(8,128)S(1)}, u32[]{:S(2)}, u32[]{:S(2)}) collective-permute-start(f32[72,128]{1,0:T(8,128)S(1)} %get-tuple-element.13), channel_id=1, source_target_pairs={{0,7},{1,6},{2,5},{3,4},{4,3},{5,2},{6,1},{7,0},{8,15},{9,14},{10,... | collective-permute-start | bytes 110600 | tf_op jit(solution)/shard_map/ppermute | solution.py:179
  11.6 3.8 %collective-permute-start.2 = (f32[72,128]{1,0:T(8,128)S(1)}, f32[72,128]{1,0:T(8,128)S(1)}, u32[]{:S(2)}, u32[]{:S(2)}) collective-permute-start(f32[72,128]{1,0:T(8,128)S(1)} %get-tuple-element.14), channel_id=1, source_target_pairs={{0,5},{1,4},{2,7},{3,6},{4,1},{5,0},{6,3},{7,2},{8,13},{9,12},{10,... | collective-permute-start | bytes 110600 | tf_op jit(solution)/shard_map/ppermute | solution.py:179
  15.4 4.8 %collective-permute-start.6 = (f32[72,128]{1,0:T(8,128)S(1)}, f32[72,128]{1,0:T(8,128)S(1)}, u32[]{:S(2)}, u32[]{:S(2)}) collective-permute-start(f32[72,128]{1,0:T(8,128)S(1)} %add_add_fusion.2), channel_id=1, source_target_pairs={{0,28},{1,29},{2,30},{3,31},{4,24},{5,25},{6,26},{7,27},{8,20},{9,... | collective-permute-start | bytes 110600 | tf_op jit(solution)/shard_map/ppermute | solution.py:179
  18.5 3.6 %collective-permute-start.5 = (f32[72,128]{1,0:T(8,128)S(1)}, f32[72,128]{1,0:T(8,128)S(1)}, u32[]{:S(2)}, u32[]{:S(2)}) collective-permute-start(f32[72,128]{1,0:T(8,128)S(1)} %add_add_fusion.2), channel_id=1, source_target_pairs={{0,12},{1,13},{2,14},{3,15},{4,8},{5,9},{6,10},{7,11},{8,4},{9,5},... | collective-permute-start | bytes 110600 | tf_op jit(solution)/shard_map/ppermute | solution.py:179
  18.5 4.3 %collective-permute-start.4 = (f32[72,128]{1,0:T(8,128)S(1)}, f32[72,128]{1,0:T(8,128)S(1)}, u32[]{:S(2)}, u32[]{:S(2)}) collective-permute-start(f32[72,128]{1,0:T(8,128)S(1)} %add_add_fusion.2), channel_id=1, source_target_pairs={{0,16},{1,17},{2,18},{3,19},{4,20},{5,21},{6,22},{7,23},{8,24},{9,... | collective-permute-start | bytes 110600 | tf_op jit(solution)/shard_map/ppermute | solution.py:179
  22.8 8.6 %collective-permute-start.7 = (f32[72,128]{1,0:T(8,128)S(1)}, f32[72,128]{1,0:T(8,128)S(1)}, u32[]{:S(2)}, u32[]{:S(2)}) collective-permute-start(f32[72,128]{1,0:T(8,128)S(1)} %add_add_fusion.1), channel_id=1, source_target_pairs={{0,228},{1,229},{2,230},{3,231},{4,224},{5,225},{6,226},{7,227},{8... | collective-permute-start | bytes 110600 | tf_op jit(solution)/shard_map/ppermute | solution.py:179
  31.4 5.3 %collective-permute-start.10 = (f32[72,128]{1,0:T(8,128)S(1)}, f32[72,128]{1,0:T(8,128)S(1)}, u32[]{:S(2)}, u32[]{:S(2)}) collective-permute-start(f32[72,128]{1,0:T(8,128)S(1)} %add.71), channel_id=1, source_target_pairs={{0,100},{1,101},{2,102},{3,103},{4,96},{5,97},{6,98},{7,99},{8,108... | collective-permute-start | bytes 110600 | tf_op jit(solution)/shard_map/ppermute | solution.py:179
  33.2 4.3 %collective-permute-start.9 = (f32[72,128]{1,0:T(8,128)S(1)}, f32[72,128]{1,0:T(8,128)S(1)}, u32[]{:S(2)}, u32[]{:S(2)}) collective-permute-start(f32[72,128]{1,0:T(8,128)S(1)} %add.71), channel_id=1, source_target_pairs={{0,36},{1,37},{2,38},{3,39},{4,32},{5,33},{6,34},{7,35},{8,44},{9,... | collective-permute-start | bytes 110600 | tf_op jit(solution)/shard_map/ppermute | solution.py:179
  34.1 3.7 %collective-permute-start.8 = (f32[72,128]{1,0:T(8,128)S(1)}, f32[72,128]{1,0:T(8,128)S(1)}, u32[]{:S(2)}, u32[]{:S(2)}) collective-permute-start(f32[72,128]{1,0:T(8,128)S(1)} %add.71), channel_id=1, source_target_pairs={{0,64},{1,65},{2,66},{3,67},{4,68},{5,69},{6,70},{7,71},{8,72},{9,... | collective-permute-start | bytes 110600 | tf_op jit(solution)/shard_map/ppermute | solution.py:179
  37.8 4.7 %collective-permute-start.13 = (f32[72,128]{1,0:T(8,128)S(1)}, f32[72,128]{1,0:T(8,128)S(1)}, u32[]{:S(2)}, u32[]{:S(2)}) collective-permute-start(f32[72,128]{1,0:T(8,128)S(1)} %add_add_fusion), channel_id=1, source_target_pairs={{0,7},{1,6},{2,5},{3,4},{4,3},{5,2},{6,1},{7,0},{8,15},{9,14},{10,... | collective-permute-start | bytes 110600 | tf_op jit(solution)/shard_map/ppermute | solution.py:179
  40.4 4.3 %collective-permute-start.12 = (f32[72,128]{1,0:T(8,128)S(1)}, f32[72,128]{1,0:T(8,128)S(1)}, u32[]{:S(2)}, u32[]{:S(2)}) collective-permute-start(f32[72,128]{1,0:T(8,128)S(1)} %add_add_fusion), channel_id=1, source_target_pairs={{0,2},{1,3},{2,0},{3,1},{4,6},{5,7},{6,4},{7,5},{8,10},{9,11},{10,... | collective-permute-start | bytes 110600 | tf_op jit(solution)/shard_map/ppermute | solution.py:179
  40.6 4.1 %collective-permute-start.11 = (f32[72,128]{1,0:T(8,128)S(1)}, f32[72,128]{1,0:T(8,128)S(1)}, u32[]{:S(2)}, u32[]{:S(2)}) collective-permute-start(f32[72,128]{1,0:T(8,128)S(1)} %add_add_fusion), channel_id=1, source_target_pairs={{0,5},{1,4},{2,7},{3,6},{4,1},{5,0},{6,3},{7,2},{8,13},{9,12},{10,... | collective-permute-start | bytes 110600 | tf_op jit(solution)/shard_map/ppermute | solution.py:179
  44.8 1.8 %collective-permute-start.14 = (f32[288,128]{1,0:T(8,128)S(1)}, f32[288,128]{1,0:T(8,128)S(1)}, u32[]{:S(2)}, u32[]{:S(2)}) collective-permute-start(f32[288,128]{1,0:T(8,128)S(1)} %pad_maximum_fusion.1), channel_id=1, source_target_pairs={{0,4},{4,0},{8,12},{12,8},{16,20},{20,16},{24,28},{28,24},{32,36},... | collective-permute-start | bytes 442376 | tf_op jit(solution)/shard_map/ppermute | solution.py:183

commit v6 on v5

--- a/solution.py
+++ b/solution.py
@@ -8,7 +8,7 @@
 BLOCK = 8
 PANEL = 2 * BLOCK
 GROUP = 16
-TILE = 256
+TILE = 512
 LIMIT = 51 * 1024 * 1024
 
 

time: 56.9 us -> 56.8 us (level)
  no operation moved by 1% of the time
where the time goes in v6:
time: 56.8 us; the launch traced here: 56.7 us
  starting transfers between devices  26.2 us (46%)
  waiting for transfers between devices  15.5 us (27%)
  Pallas kernels  13.9 us (24%)
  between operations  0.92 us (2%)
    ppermute x13, starting transfers between devices, flip(): return lax.ppermute(x, ('rows', 'batch'), pairs)  22.1 us
    ppermute x13, waiting for transfers between devices, flip(): return lax.ppermute(x, ('rows', 'batch'), pairs)  13.5 us
    pallas_call x1, Pallas kernels, shards(): pl.pallas_call(lambda *refs: modes_kernel(1.0 / stack, planes, width, *re...  9.89 us
    ppermute x2, starting transfers between devices, other_core(): lax.ppermute(x, 'rows', [(i, i ^ 1) for i in range(lax.axis_size('rows'))])  4.13 us
    pallas_call x1, Pallas kernels, shards(): pl.pallas_call(lambda *refs: gram_kernel(planes, width, *refs), in_specs=...  3.97 us
    ppermute x2, waiting for transfers between devices, other_core(): lax.ppermute(x, 'rows', [(i, i ^ 1) for i in range(lax.axis_size('rows'))])  2.01 us
  transfers between devices with their start and end apart: 15, of which 13 were waited for; matrix products, arithmetic and copies ran while one was open for 0% of the time, Pallas kernels for 0%

profile of v6, /device:TPU:1, one launch (start us, length us, event | category | flops | bytes accessed | tf_op | source)
XLA Modules:
  0.0 56.7 jit_solution(2498379685803495117)
XLA Ops:
  0.7 4.0 %gram.1 = f32[576,128]{1,0:T(8,128)S(1)} custom-call(bf16[8,2048,128]{2,1,0:T(8,128)(2,1)} %refs_1_.1), custom_call_target="tpu_custom_call" | custom-call | tf_op jit(solution)/shard_map/gram/pallas_call | solution.py:219
  4.7 3.3 %collective-permute-start = (f32[288,128]{1,0:T(8,128)S(1)}, f32[288,128]{1,0:T(8,128)S(1)}, u32[]{:S(2)}, u32[]{:S(2)}) collective-permute-start(f32[288,128]{1,0:T(8,128)S(1)} %constant_dynamic-slice_fusion.3), channel_id=1, source_target_pairs={{0,4},{4,0},{8,12},{12,8},{16,20},{20,16},{24,28},{28,24},{32,36},... | collective-permute-start | bytes 442376 | tf_op jit(solution)/shard_map/ppermute | solution.py:183
  8.0 1.0 %collective-permute-done = f32[288,128]{1,0:T(8,128)S(1)} collective-permute-done((f32[288,128]{1,0:T(8,128)S(1)}, f32[288,128]{1,0:T(8,128)S(1)}, u32[]{:S(2)}, u32[]{:S(2)}) %collective-permute-start) | collective-permute-done | bytes 147488 | tf_op jit(solution)/shard_map/ppermute | solution.py:183
  9.1 1.1 %collective-permute-start.1 = (f32[72,128]{1,0:T(8,128)S(1)}, f32[72,128]{1,0:T(8,128)S(1)}, u32[]{:S(2)}, u32[]{:S(2)}) collective-permute-start(f32[72,128]{1,0:T(8,128)S(1)} %get-tuple-element.12), channel_id=1, source_target_pairs={{0,2},{1,3},{2,0},{3,1},{4,6},{5,7},{6,4},{7,5},{8,10},{9,11},{10,... | collective-permute-start | bytes 110600 | tf_op jit(solution)/shard_map/ppermute | solution.py:179
  10.2 1.4 %collective-permute-start.3 = (f32[72,128]{1,0:T(8,128)S(1)}, f32[72,128]{1,0:T(8,128)S(1)}, u32[]{:S(2)}, u32[]{:S(2)}) collective-permute-start(f32[72,128]{1,0:T(8,128)S(1)} %get-tuple-element.13), channel_id=1, source_target_pairs={{0,7},{1,6},{2,5},{3,4},{4,3},{5,2},{6,1},{7,0},{8,15},{9,14},{10,... | collective-permute-start | bytes 110600 | tf_op jit(solution)/shard_map/ppermute | solution.py:179
  11.6 0.5 collective-permute-start.2
  12.1 1.4 %collective-permute-done.1 = f32[72,128]{1,0:T(8,128)S(1)} collective-permute-done((f32[72,128]{1,0:T(8,128)S(1)}, f32[72,128]{1,0:T(8,128)S(1)}, u32[]{:S(2)}, u32[]{:S(2)}) %collective-permute-start.1) | collective-permute-done | bytes 36896 | tf_op jit(solution)/shard_map/ppermute | solution.py:179
  13.5 1.9 %collective-permute-done.3 = f32[72,128]{1,0:T(8,128)S(1)} collective-permute-done((f32[72,128]{1,0:T(8,128)S(1)}, f32[72,128]{1,0:T(8,128)S(1)}, u32[]{:S(2)}, u32[]{:S(2)}) %collective-permute-start.3) | collective-permute-done | bytes 36896 | tf_op jit(solution)/shard_map/ppermute | solution.py:179
  15.4 0.0 collective-permute-done.2
  15.4 3.1 %collective-permute-start.6 = (f32[72,128]{1,0:T(8,128)S(1)}, f32[72,128]{1,0:T(8,128)S(1)}, u32[]{:S(2)}, u32[]{:S(2)}) collective-permute-start(f32[72,128]{1,0:T(8,128)S(1)} %add_add_fusion.2), channel_id=1, source_target_pairs={{0,28},{1,29},{2,30},{3,31},{4,24},{5,25},{6,26},{7,27},{8,20},{9,... | collective-permute-start | bytes 110600 | tf_op jit(solution)/shard_map/ppermute | solution.py:179
  18.5 0.0 collective-permute-start.5
  18.5 1.3 %collective-permute-start.4 = (f32[72,128]{1,0:T(8,128)S(1)}, f32[72,128]{1,0:T(8,128)S(1)}, u32[]{:S(2)}, u32[]{:S(2)}) collective-permute-start(f32[72,128]{1,0:T(8,128)S(1)} %add_add_fusion.2), channel_id=1, source_target_pairs={{0,16},{1,17},{2,18},{3,19},{4,20},{5,21},{6,22},{7,23},{8,24},{9,... | collective-permute-start | bytes 110600 | tf_op jit(solution)/shard_map/ppermute | solution.py:179
  19.8 0.4 collective-permute-done.6
  20.2 1.9 %collective-permute-done.5 = f32[72,128]{1,0:T(8,128)S(1)} collective-permute-done((f32[72,128]{1,0:T(8,128)S(1)}, f32[72,128]{1,0:T(8,128)S(1)}, u32[]{:S(2)}, u32[]{:S(2)}) %collective-permute-start.5) | collective-permute-done | bytes 36896 | tf_op jit(solution)/shard_map/ppermute | solution.py:179
  22.1 0.7 %collective-permute-done.4 = f32[72,128]{1,0:T(8,128)S(1)} collective-permute-done((f32[72,128]{1,0:T(8,128)S(1)}, f32[72,128]{1,0:T(8,128)S(1)}, u32[]{:S(2)}, u32[]{:S(2)}) %collective-permute-start.4) | collective-permute-done | bytes 36896 | tf_op jit(solution)/shard_map/ppermute | solution.py:179
  22.8 7.0 %collective-permute-start.7 = (f32[72,128]{1,0:T(8,128)S(1)}, f32[72,128]{1,0:T(8,128)S(1)}, u32[]{:S(2)}, u32[]{:S(2)}) collective-permute-start(f32[72,128]{1,0:T(8,128)S(1)} %add_add_fusion.1), channel_id=1, source_target_pairs={{0,228},{1,229},{2,230},{3,231},{4,224},{5,225},{6,226},{7,227},{8... | collective-permute-start | bytes 110600 | tf_op jit(solution)/shard_map/ppermute | solution.py:179
  29.8 1.6 %collective-permute-done.7 = f32[72,128]{1,0:T(8,128)S(1)} collective-permute-done((f32[72,128]{1,0:T(8,128)S(1)}, f32[72,128]{1,0:T(8,128)S(1)}, u32[]{:S(2)}, u32[]{:S(2)}) %collective-permute-start.7) | collective-permute-done | bytes 36896 | tf_op jit(solution)/shard_map/ppermute | solution.py:179
  31.4 1.7 %collective-permute-start.10 = (f32[72,128]{1,0:T(8,128)S(1)}, f32[72,128]{1,0:T(8,128)S(1)}, u32[]{:S(2)}, u32[]{:S(2)}) collective-permute-start(f32[72,128]{1,0:T(8,128)S(1)} %add.71), channel_id=1, source_target_pairs={{0,100},{1,101},{2,102},{3,103},{4,96},{5,97},{6,98},{7,99},{8,108... | collective-permute-start | bytes 110600 | tf_op jit(solution)/shard_map/ppermute | solution.py:179
  33.2 1.0 %collective-permute-start.9 = (f32[72,128]{1,0:T(8,128)S(1)}, f32[72,128]{1,0:T(8,128)S(1)}, u32[]{:S(2)}, u32[]{:S(2)}) collective-permute-start(f32[72,128]{1,0:T(8,128)S(1)} %add.71), channel_id=1, source_target_pairs={{0,36},{1,37},{2,38},{3,39},{4,32},{5,33},{6,34},{7,35},{8,44},{9,... | collective-permute-start | bytes 110600 | tf_op jit(solution)/shard_map/ppermute | solution.py:179
  34.1 1.1 %collective-permute-start.8 = (f32[72,128]{1,0:T(8,128)S(1)}, f32[72,128]{1,0:T(8,128)S(1)}, u32[]{:S(2)}, u32[]{:S(2)}) collective-permute-start(f32[72,128]{1,0:T(8,128)S(1)} %add.71), channel_id=1, source_target_pairs={{0,64},{1,65},{2,66},{3,67},{4,68},{5,69},{6,70},{7,71},{8,72},{9,... | collective-permute-start | bytes 110600 | tf_op jit(solution)/shard_map/ppermute | solution.py:179
  35.3 1.5 %collective-permute-done.10 = f32[72,128]{1,0:T(8,128)S(1)} collective-permute-done((f32[72,128]{1,0:T(8,128)S(1)}, f32[72,128]{1,0:T(8,128)S(1)}, u32[]{:S(2)}, u32[]{:S(2)}) %collective-permute-start.10) | collective-permute-done | bytes 36896 | tf_op jit(solution)/shard_map/ppermute | solution.py:179
  36.7 0.7 %collective-permute-done.9 = f32[72,128]{1,0:T(8,128)S(1)} collective-permute-done((f32[72,128]{1,0:T(8,128)S(1)}, f32[72,128]{1,0:T(8,128)S(1)}, u32[]{:S(2)}, u32[]{:S(2)}) %collective-permute-start.9) | collective-permute-done | bytes 36896 | tf_op jit(solution)/shard_map/ppermute | solution.py:179
  37.5 0.4 collective-permute-done.8
  37.8 2.5 %collective-permute-start.13 = (f32[72,128]{1,0:T(8,128)S(1)}, f32[72,128]{1,0:T(8,128)S(1)}, u32[]{:S(2)}, u32[]{:S(2)}) collective-permute-start(f32[72,128]{1,0:T(8,128)S(1)} %add_add_fusion), channel_id=1, source_target_pairs={{0,7},{1,6},{2,5},{3,4},{4,3},{5,2},{6,1},{7,0},{8,15},{9,14},{10,... | collective-permute-start | bytes 110600 | tf_op jit(solution)/shard_map/ppermute | solution.py:179
  40.4 0.2 collective-permute-start.12
  40.6 1.1 %collective-permute-start.11 = (f32[72,128]{1,0:T(8,128)S(1)}, f32[72,128]{1,0:T(8,128)S(1)}, u32[]{:S(2)}, u32[]{:S(2)}) collective-permute-start(f32[72,128]{1,0:T(8,128)S(1)} %add_add_fusion), channel_id=1, source_target_pairs={{0,5},{1,4},{2,7},{3,6},{4,1},{5,0},{6,3},{7,2},{8,13},{9,12},{10,... | collective-permute-start | bytes 110600 | tf_op jit(solution)/shard_map/ppermute | solution.py:179
  41.7 0.8 %collective-permute-done.13 = f32[72,128]{1,0:T(8,128)S(1)} collective-permute-done((f32[72,128]{1,0:T(8,128)S(1)}, f32[72,128]{1,0:T(8,128)S(1)}, u32[]{:S(2)}, u32[]{:S(2)}) %collective-permute-start.13) | collective-permute-done | bytes 36896 | tf_op jit(solution)/shard_map/ppermute | solution.py:179
  42.5 2.2 %collective-permute-done.12 = f32[72,128]{1,0:T(8,128)S(1)} collective-permute-done((f32[72,128]{1,0:T(8,128)S(1)}, f32[72,128]{1,0:T(8,128)S(1)}, u32[]{:S(2)}, u32[]{:S(2)}) %collective-permute-start.12) | collective-permute-done | bytes 36896 | tf_op jit(solution)/shard_map/ppermute | solution.py:179
  44.7 0.0 collective-permute-done.11
  44.8 0.8 %collective-permute-start.14 = (f32[288,128]{1,0:T(8,128)S(1)}, f32[288,128]{1,0:T(8,128)S(1)}, u32[]{:S(2)}, u32[]{:S(2)}) collective-permute-start(f32[288,128]{1,0:T(8,128)S(1)} %pad_maximum_fusion.1), channel_id=1, source_target_pairs={{0,4},{4,0},{8,12},{12,8},{16,20},{20,16},{24,28},{28,24},{32,36},... | collective-permute-start | bytes 442376 | tf_op jit(solution)/shard_map/ppermute | solution.py:183
  45.6 1.0 %collective-permute-done.14 = f32[288,128]{1,0:T(8,128)S(1)} collective-permute-done((f32[288,128]{1,0:T(8,128)S(1)}, f32[288,128]{1,0:T(8,128)S(1)}, u32[]{:S(2)}, u32[]{:S(2)}) %collective-permute-start.14) | collective-permute-done | bytes 147488 | tf_op jit(solution)/shard_map/ppermute | solution.py:183
  46.6 9.9 %factor_modes.1 = (f32[1024,128]{1,0:T(8,128)}, f32[8,2048,128]{2,1,0:T(8,128)}) custom-call(f32[576,128]{1,0:T(8,128)S(1)} %pad_maximum_fusion.refs_0_, bf16[8,2048,128]{2,1,0:T(8,128)(2,1)} %refs_1_.1), custom_call_target="tpu_custom_call" | custom-call | tf_op jit(solution)/shard_map/factor_modes/pallas_call | solution.py:233
  (11 shorter events, 0.2 us)
Async XLA Ops:
  4.7 4.3 %collective-permute-start = (f32[288,128]{1,0:T(8,128)S(1)}, f32[288,128]{1,0:T(8,128)S(1)}, u32[]{:S(2)}, u32[]{:S(2)}) collective-permute-start(f32[288,128]{1,0:T(8,128)S(1)} %constant_dynamic-slice_fusion.3), channel_id=1, source_target_pairs={{0,4},{4,0},{8,12},{12,8},{16,20},{20,16},{24,28},{28,24},{32,36},... | collective-permute-start | bytes 442376 | tf_op jit(solution)/shard_map/ppermute | solution.py:183
  9.1 4.4 %collective-permute-start.1 = (f32[72,128]{1,0:T(8,128)S(1)}, f32[72,128]{1,0:T(8,128)S(1)}, u32[]{:S(2)}, u32[]{:S(2)}) collective-permute-start(f32[72,128]{1,0:T(8,128)S(1)} %get-tuple-element.12), channel_id=1, source_target_pairs={{0,2},{1,3},{2,0},{3,1},{4,6},{5,7},{6,4},{7,5},{8,10},{9,11},{10,... | collective-permute-start | bytes 110600 | tf_op jit(solution)/shard_map/ppermute | solution.py:179
  10.2 5.2 %collective-permute-start.3 = (f32[72,128]{1,0:T(8,128)S(1)}, f32[72,128]{1,0:T(8,128)S(1)}, u32[]{:S(2)}, u32[]{:S(2)}) collective-permute-start(f32[72,128]{1,0:T(8,128)S(1)} %get-tuple-element.13), channel_id=1, source_target_pairs={{0,7},{1,6},{2,5},{3,4},{4,3},{5,2},{6,1},{7,0},{8,15},{9,14},{10,... | collective-permute-start | bytes 110600 | tf_op jit(solution)/shard_map/ppermute | solution.py:179
  11.6 3.8 %collective-permute-start.2 = (f32[72,128]{1,0:T(8,128)S(1)}, f32[72,128]{1,0:T(8,128)S(1)}, u32[]{:S(2)}, u32[]{:S(2)}) collective-permute-start(f32[72,128]{1,0:T(8,128)S(1)} %get-tuple-element.14), channel_id=1, source_target_pairs={{0,5},{1,4},{2,7},{3,6},{4,1},{5,0},{6,3},{7,2},{8,13},{9,12},{10,... | collective-permute-start | bytes 110600 | tf_op jit(solution)/shard_map/ppermute | solution.py:179
  15.4 4.8 %collective-permute-start.6 = (f32[72,128]{1,0:T(8,128)S(1)}, f32[72,128]{1,0:T(8,128)S(1)}, u32[]{:S(2)}, u32[]{:S(2)}) collective-permute-start(f32[72,128]{1,0:T(8,128)S(1)} %add_add_fusion.2), channel_id=1, source_target_pairs={{0,28},{1,29},{2,30},{3,31},{4,24},{5,25},{6,26},{7,27},{8,20},{9,... | collective-permute-start | bytes 110600 | tf_op jit(solution)/shard_map/ppermute | solution.py:179
  18.5 3.6 %collective-permute-start.5 = (f32[72,128]{1,0:T(8,128)S(1)}, f32[72,128]{1,0:T(8,128)S(1)}, u32[]{:S(2)}, u32[]{:S(2)}) collective-permute-start(f32[72,128]{1,0:T(8,128)S(1)} %add_add_fusion.2), channel_id=1, source_target_pairs={{0,12},{1,13},{2,14},{3,15},{4,8},{5,9},{6,10},{7,11},{8,4},{9,5},... | collective-permute-start | bytes 110600 | tf_op jit(solution)/shard_map/ppermute | solution.py:179
  18.5 4.3 %collective-permute-start.4 = (f32[72,128]{1,0:T(8,128)S(1)}, f32[72,128]{1,0:T(8,128)S(1)}, u32[]{:S(2)}, u32[]{:S(2)}) collective-permute-start(f32[72,128]{1,0:T(8,128)S(1)} %add_add_fusion.2), channel_id=1, source_target_pairs={{0,16},{1,17},{2,18},{3,19},{4,20},{5,21},{6,22},{7,23},{8,24},{9,... | collective-permute-start | bytes 110600 | tf_op jit(solution)/shard_map/ppermute | solution.py:179
  22.8 8.6 %collective-permute-start.7 = (f32[72,128]{1,0:T(8,128)S(1)}, f32[72,128]{1,0:T(8,128)S(1)}, u32[]{:S(2)}, u32[]{:S(2)}) collective-permute-start(f32[72,128]{1,0:T(8,128)S(1)} %add_add_fusion.1), channel_id=1, source_target_pairs={{0,228},{1,229},{2,230},{3,231},{4,224},{5,225},{6,226},{7,227},{8... | collective-permute-start | bytes 110600 | tf_op jit(solution)/shard_map/ppermute | solution.py:179
  31.4 5.3 %collective-permute-start.10 = (f32[72,128]{1,0:T(8,128)S(1)}, f32[72,128]{1,0:T(8,128)S(1)}, u32[]{:S(2)}, u32[]{:S(2)}) collective-permute-start(f32[72,128]{1,0:T(8,128)S(1)} %add.71), channel_id=1, source_target_pairs={{0,100},{1,101},{2,102},{3,103},{4,96},{5,97},{6,98},{7,99},{8,108... | collective-permute-start | bytes 110600 | tf_op jit(solution)/shard_map/ppermute | solution.py:179
  33.2 4.3 %collective-permute-start.9 = (f32[72,128]{1,0:T(8,128)S(1)}, f32[72,128]{1,0:T(8,128)S(1)}, u32[]{:S(2)}, u32[]{:S(2)}) collective-permute-start(f32[72,128]{1,0:T(8,128)S(1)} %add.71), channel_id=1, source_target_pairs={{0,36},{1,37},{2,38},{3,39},{4,32},{5,33},{6,34},{7,35},{8,44},{9,... | collective-permute-start | bytes 110600 | tf_op jit(solution)/shard_map/ppermute | solution.py:179
  34.1 3.7 %collective-permute-start.8 = (f32[72,128]{1,0:T(8,128)S(1)}, f32[72,128]{1,0:T(8,128)S(1)}, u32[]{:S(2)}, u32[]{:S(2)}) collective-permute-start(f32[72,128]{1,0:T(8,128)S(1)} %add.71), channel_id=1, source_target_pairs={{0,64},{1,65},{2,66},{3,67},{4,68},{5,69},{6,70},{7,71},{8,72},{9,... | collective-permute-start | bytes 110600 | tf_op jit(solution)/shard_map/ppermute | solution.py:179
  37.8 4.7 %collective-permute-start.13 = (f32[72,128]{1,0:T(8,128)S(1)}, f32[72,128]{1,0:T(8,128)S(1)}, u32[]{:S(2)}, u32[]{:S(2)}) collective-permute-start(f32[72,128]{1,0:T(8,128)S(1)} %add_add_fusion), channel_id=1, source_target_pairs={{0,7},{1,6},{2,5},{3,4},{4,3},{5,2},{6,1},{7,0},{8,15},{9,14},{10,... | collective-permute-start | bytes 110600 | tf_op jit(solution)/shard_map/ppermute | solution.py:179
  40.4 4.3 %collective-permute-start.12 = (f32[72,128]{1,0:T(8,128)S(1)}, f32[72,128]{1,0:T(8,128)S(1)}, u32[]{:S(2)}, u32[]{:S(2)}) collective-permute-start(f32[72,128]{1,0:T(8,128)S(1)} %add_add_fusion), channel_id=1, source_target_pairs={{0,2},{1,3},{2,0},{3,1},{4,6},{5,7},{6,4},{7,5},{8,10},{9,11},{10,... | collective-permute-start | bytes 110600 | tf_op jit(solution)/shard_map/ppermute | solution.py:179
  40.6 4.1 %collective-permute-start.11 = (f32[72,128]{1,0:T(8,128)S(1)}, f32[72,128]{1,0:T(8,128)S(1)}, u32[]{:S(2)}, u32[]{:S(2)}) collective-permute-start(f32[72,128]{1,0:T(8,128)S(1)} %add_add_fusion), channel_id=1, source_target_pairs={{0,5},{1,4},{2,7},{3,6},{4,1},{5,0},{6,3},{7,2},{8,13},{9,12},{10,... | collective-permute-start | bytes 110600 | tf_op jit(solution)/shard_map/ppermute | solution.py:179
  44.8 1.8 %collective-permute-start.14 = (f32[288,128]{1,0:T(8,128)S(1)}, f32[288,128]{1,0:T(8,128)S(1)}, u32[]{:S(2)}, u32[]{:S(2)}) collective-permute-start(f32[288,128]{1,0:T(8,128)S(1)} %pad_maximum_fusion.1), channel_id=1, source_target_pairs={{0,4},{4,0},{8,12},{12,8},{16,20},{20,16},{24,28},{28,24},{32,36},... | collective-permute-start | bytes 442376 | tf_op jit(solution)/shard_map/ppermute | solution.py:183
